TPU v7x, 256 devices: a whole 4x4x8 slice. The times are simulated.
256 devices in a mesh: blk: 32 (over x_lo, z, core), col: 8 (over y, x_hi).
Axes of the slice: x: 4 (x_hi: 2, x_lo: 2; x = x_hi * 2 + x_lo), y: 4, z: 8, core: 2. Of those that a mesh axis runs over, the one named last changes fastest.
Arguments:
- images: float32 [1152, 16384], P('col', 'blk'), may hold values from -0.8 to 0.8
- texts: float32 [1152, 16384], P('col', 'blk'), may hold values from -0.8 to 0.8
- log_temp: float32 [1], replicated, may hold values from 1.6 to 2.6
- bias: float32 [1], replicated, may hold values from -3 to -1
Outputs:
- loss: float32 [1], replicated
- grad_images: float32 [1152, 16384], P('col', 'blk')
- grad_texts: float32 [1152, 16384], P('col', 'blk')
- grad_log_temp: float32 [1], replicated
- grad_bias: float32 [1], replicated
All inputs are finite; a program needn't handle non-finite values.
Results may differ from a plain program's by a relative error of at most 0.00035.
The roundings to bfloat16 on the way count: a program that leaves them out, or rounds other values in their place, can miss the bound.
Values may be sent and summed in bfloat16 or wider, within the bound.
A program may use at most 64 MiB of HBM per device.

v0:
```python
import jax
import jax.numpy as jnp
from jax import lax
from jax.sharding import PartitionSpec as P

epsilon = 1e-06


def passed_along(value, axis, by):
    size = lax.axis_size(axis)
    return lax.ppermute(value, axis, [(i, (i + by) % size) for i in range(size)])


def normalize(values):
    scale = lax.rsqrt(jnp.sum(values * values, axis=1, keepdims=True) + epsilon)
    return (values * scale, scale)


def tile_terms(image_low, text_block, anchor, row_offset, own_index, temper, bias_value):
    row_count = text_block.shape[0]
    image_count = image_low.shape[0]
    scores = lax.dot_general(
        text_block, image_low, (((1,), (1,)), ((), ())), preferred_element_type=jnp.float32
    )
    text_pos = anchor * image_count + row_offset + jnp.arange(row_count, dtype=jnp.int32)
    image_pos = own_index * image_count + jnp.arange(image_count, dtype=jnp.int32)
    labels = jnp.where(text_pos[:, None] == image_pos[None, :], 1.0, -1.0).astype(jnp.float32)
    logits = temper * scores + bias_value
    losses = jax.nn.softplus(-labels * logits)
    slopes = -labels * jax.nn.sigmoid(-labels * logits)
    weighted = (temper * slopes).astype(jnp.bfloat16)
    image_part = lax.dot_general(
        weighted, text_block, (((0,), (0,)), ((), ())), preferred_element_type=jnp.float32
    )
    text_part = jnp.dot(weighted, image_low, preferred_element_type=jnp.float32)
    sums = jnp.stack([jnp.sum(losses), jnp.sum(slopes * scores) * temper, jnp.sum(slopes)])
    return (image_part, text_part, sums)


def per_device(images, texts, log_temp, bias):
    own_index = lax.axis_index("blk")
    cycle_size = lax.axis_size("blk")
    col_index = lax.axis_index("col")
    image_rows = lax.all_gather(images, "col", axis=0, tiled=True).T
    image_unit, image_scale = normalize(image_rows)
    image_low = image_unit.astype(jnp.bfloat16)
    text_rows = lax.all_to_all(texts, "col", split_axis=1, concat_axis=0, tiled=True).T
    text_unit, text_scale = normalize(text_rows)
    text_low = text_unit.astype(jnp.bfloat16)
    temper = jnp.exp(log_temp[0])
    bias_value = bias[0]
    text_count = text_rows.shape[0]
    width = text_rows.shape[1]
    image_count = image_rows.shape[0]
    row_offset = col_index * text_count
    zero_image = jnp.zeros((image_count, width), jnp.float32)
    zero_sums = jnp.zeros((3,), jnp.float32)

    def turn(turn_index, carried):
        text_block, text_grads, image_grads, totals = carried
        anchor = (own_index - turn_index) % cycle_size
        image_part, text_part, sums = tile_terms(
            image_low, text_block, anchor, row_offset, own_index, temper, bias_value
        )
        text_block, text_grads = (
            passed_along(text_block.astype(jnp.float32), "blk", 1).astype(text_block.dtype),
            passed_along(text_grads + text_part, "blk", 1),
        )
        return (text_block, text_grads, image_grads + image_part, totals + sums)

    start = (text_low, jnp.zeros((text_count, width), jnp.float32), zero_image, zero_sums)
    moved, text_grads, image_grads, totals = lax.fori_loop(0, cycle_size, turn, start)
    share_width = images.shape[0]
    whole_grads = lax.psum(image_grads, "col")
    full_grads = image_scale * (
        whole_grads - image_unit * jnp.sum(image_unit * whole_grads, axis=1, keepdims=True)
    )
    grad_images = lax.dynamic_slice_in_dim(full_grads.T, col_index * share_width, share_width, 0)
    text_full = text_scale * (
        text_grads - text_unit * jnp.sum(text_unit * text_grads, axis=1, keepdims=True)
    )
    grad_texts = lax.all_to_all(text_full.T, "col", split_axis=0, concat_axis=1, tiled=True)
    sums_all = lax.psum(totals, ("blk", "col"))
    total_rows = jnp.float32(image_count * cycle_size)
    pairs = total_rows * total_rows
    loss = jnp.reshape(sums_all[0] / pairs, (1,))
    grad_log_temp = jnp.reshape(sums_all[1] / pairs, (1,))
    grad_bias = jnp.reshape(sums_all[2] / pairs, (1,))
    return (loss, grad_images, grad_texts, grad_log_temp, grad_bias)


def solution(mesh):
    in_specs = (P("col", "blk"), P("col", "blk"), P(), P())
    out_specs = (P(), P("col", "blk"), P("col", "blk"), P(), P())
    return jax.shard_map(
        per_device, mesh=mesh, in_specs=in_specs, out_specs=out_specs, check_vma=False
    )
```

profile of v0, /device:TPU:2, one launch (start us, length us, event | category | flops | bytes accessed | tf_op | source)
XLA Modules:
  0.0 747.6 jit_solution(18110613993056820326)
XLA Ops:
  9.9 6.0 all-to-all-start
  16.7 10.8 %all-to-all-done = f32[144,8,64]{0,2,1:T(8,128)S(1)} async-done(((f32[144,8,64]{0,2,1:T(8,128)}), f32[144,8,64]{0,2,1:T(8,128)S(1)}, u32[]{:S(2)}, u32[]{:S(2)}) %all-to-all-start) | async-done | bytes 294944 | tf_op jit(solution)/shard_map/all_to_all | solution.py:47
  28.9 45.1 %all-gather.2.cloned.1.call-done = f32[1152,512]{1,0:T(8,128)} async-done(((f32[144,512]{1,0:T(8,128)}), f32[1152,512]{1,0:T(8,128)}) %all-gather.2.cloned.1.call-update) | async-done | bytes 2359312 | tf_op jit(solution)/shard_map/all_gather | solution.py:44
  80.9 523.7 %while.22 = (s32[]{:T(128)}, bf16[64,1152]{1,0:T(8,128)(2,1)}, f32[64,1152]{1,0:T(8,128)}, f32[512,1152]{1,0:T(8,128)S(1)}, f32[3]{0:T(128)S(1)}, /*index=5*/f32...) while((s32[]{:T(128)}, bf16[64,1152]{1,0:T(8,128)(2,1)}, ...), condition=%wide.region_6.7_spmd.clone, body=%wide.region_2.6_spmd.clone.sunk | while | flops 229188192 | bytes 10954233 | solution.py:72
  109.9 3.7 collective-permute-done.1
  126.3 3.7 collective-permute-done.1
  142.6 3.7 collective-permute-done.1
  159.0 3.7 collective-permute-done.1
  175.4 3.7 collective-permute-done.1
  191.7 3.7 collective-permute-done.1
  208.1 3.7 collective-permute-done.1
  224.4 3.7 collective-permute-done.1
  240.8 3.7 collective-permute-done.1
  257.2 3.7 collective-permute-done.1
  273.5 3.7 collective-permute-done.1
  289.9 3.7 collective-permute-done.1
  306.3 3.7 collective-permute-done.1
  322.6 3.7 collective-permute-done.1
  339.0 3.7 collective-permute-done.1
  355.4 3.7 collective-permute-done.1
  371.7 3.7 collective-permute-done.1
  388.1 3.7 collective-permute-done.1
  404.5 3.7 collective-permute-done.1
  420.8 3.7 collective-permute-done.1
  453.6 3.7 collective-permute-done.1
  469.9 3.7 collective-permute-done.1
  502.7 3.7 collective-permute-done.1
  519.0 3.7 collective-permute-done.1
  551.8 3.7 collective-permute-done.1
  568.1 3.7 collective-permute-done.1
  600.8 3.7 collective-permute-done.1
  614.9 115.3 %psum.14 = f32[3]{0:T(128)S(1)} all-reduce(f32[3]{0:T(128)S(1)} %get-tuple-element.256), channel_id=1, replica_groups=mesh['blk'=32,'col'=8] {'blk','col'}, use_global_device_ids=true, to_apply=%region_7.8 | all-reduce | flops 3 | bytes 24 | tf_op jit(solution)/shard_map/psum | solution.py:83
  (430 shorter events, 427.3 us)
Async XLA Ops:
  7.2 66.8 %all-gather.2.cloned.1.call-start = ((), (), s32[]{:S(2)}) async-start(), calls=%async_computation.2 | async-start | bytes 2654208 | tf_op jit(solution)/shard_map/all_gather | solution.py:44
  9.9 17.6 %all-to-all-start = ((f32[144,8,64]{0,2,1:T(8,128)}), f32[144,8,64]{0,2,1:T(8,128)S(1)}, u32[]{:S(2)}, u32[]{:S(2)}) async-start(f32[144,8,64]{0,2,1:T(8,128)} %bitcast), calls=%async_computation | async-start | bytes 1048576 | tf_op jit(solution)/shard_map/all_to_all | solution.py:47
  15.9 717.7 %all-reduce.2.cloned.1.call-start = ((), (), s32[]{:S(2)}) async-start(), calls=%async_computation.3 | async-start | bytes 4718592 | tf_op jit(solution)/shard_map/psum | solution.py:74
  82.5 12.7 %collective-permute-start = (bf16[64,1152]{1,0:T(8,128)(2,1)}, bf16[64,1152]{1,0:T(8,128)(2,1)}, u32[]{:S(2)}, u32[]{:S(2)}) collective-permute-start(bf16[64,1152]{1,0:T(8,128)(2,1)} %copy.34), channel_id=1, source_target_pairs={{0,8},{8,16},{16,24},{24,32},{32,40},{40,48},{48,56},{56,64},{64,7... | collective-permute-start | bytes 442376 | tf_op jit(solution)/shard_map/while/body/eval_jaxpr/ppermute | solution.py:11
  98.8 11.0 %collective-permute-start = (bf16[64,1152]{1,0:T(8,128)(2,1)}, bf16[64,1152]{1,0:T(8,128)(2,1)}, u32[]{:S(2)}, u32[]{:S(2)}) collective-permute-start(bf16[64,1152]{1,0:T(8,128)(2,1)} %copy.34), channel_id=1, source_target_pairs={{0,8},{8,16},{16,24},{24,32},{32,40},{40,48},{48,56},{56,64},{64,7... | collective-permute-start | bytes 442376 | tf_op jit(solution)/shard_map/while/body/eval_jaxpr/ppermute | solution.py:11
  131.6 11.0 %collective-permute-start = (bf16[64,1152]{1,0:T(8,128)(2,1)}, bf16[64,1152]{1,0:T(8,128)(2,1)}, u32[]{:S(2)}, u32[]{:S(2)}) collective-permute-start(bf16[64,1152]{1,0:T(8,128)(2,1)} %copy.34), channel_id=1, source_target_pairs={{0,8},{8,16},{16,24},{24,32},{32,40},{40,48},{48,56},{56,64},{64,7... | collective-permute-start | bytes 442376 | tf_op jit(solution)/shard_map/while/body/eval_jaxpr/ppermute | solution.py:11
  147.9 11.1 %collective-permute-start = (bf16[64,1152]{1,0:T(8,128)(2,1)}, bf16[64,1152]{1,0:T(8,128)(2,1)}, u32[]{:S(2)}, u32[]{:S(2)}) collective-permute-start(bf16[64,1152]{1,0:T(8,128)(2,1)} %copy.34), channel_id=1, source_target_pairs={{0,8},{8,16},{16,24},{24,32},{32,40},{40,48},{48,56},{56,64},{64,7... | collective-permute-start | bytes 442376 | tf_op jit(solution)/shard_map/while/body/eval_jaxpr/ppermute | solution.py:11
  164.3 11.0 %collective-permute-start = (bf16[64,1152]{1,0:T(8,128)(2,1)}, bf16[64,1152]{1,0:T(8,128)(2,1)}, u32[]{:S(2)}, u32[]{:S(2)}) collective-permute-start(bf16[64,1152]{1,0:T(8,128)(2,1)} %copy.34), channel_id=1, source_target_pairs={{0,8},{8,16},{16,24},{24,32},{32,40},{40,48},{48,56},{56,64},{64,7... | collective-permute-start | bytes 442376 | tf_op jit(solution)/shard_map/while/body/eval_jaxpr/ppermute | solution.py:11
  180.7 11.0 %collective-permute-start = (bf16[64,1152]{1,0:T(8,128)(2,1)}, bf16[64,1152]{1,0:T(8,128)(2,1)}, u32[]{:S(2)}, u32[]{:S(2)}) collective-permute-start(bf16[64,1152]{1,0:T(8,128)(2,1)} %copy.34), channel_id=1, source_target_pairs={{0,8},{8,16},{16,24},{24,32},{32,40},{40,48},{48,56},{56,64},{64,7... | collective-permute-start | bytes 442376 | tf_op jit(solution)/shard_map/while/body/eval_jaxpr/ppermute | solution.py:11
  197.0 11.1 %collective-permute-start = (bf16[64,1152]{1,0:T(8,128)(2,1)}, bf16[64,1152]{1,0:T(8,128)(2,1)}, u32[]{:S(2)}, u32[]{:S(2)}) collective-permute-start(bf16[64,1152]{1,0:T(8,128)(2,1)} %copy.34), channel_id=1, source_target_pairs={{0,8},{8,16},{16,24},{24,32},{32,40},{40,48},{48,56},{56,64},{64,7... | collective-permute-start | bytes 442376 | tf_op jit(solution)/shard_map/while/body/eval_jaxpr/ppermute | solution.py:11
  213.4 11.0 %collective-permute-start = (bf16[64,1152]{1,0:T(8,128)(2,1)}, bf16[64,1152]{1,0:T(8,128)(2,1)}, u32[]{:S(2)}, u32[]{:S(2)}) collective-permute-start(bf16[64,1152]{1,0:T(8,128)(2,1)} %copy.34), channel_id=1, source_target_pairs={{0,8},{8,16},{16,24},{24,32},{32,40},{40,48},{48,56},{56,64},{64,7... | collective-permute-start | bytes 442376 | tf_op jit(solution)/shard_map/while/body/eval_jaxpr/ppermute | solution.py:11
  229.8 11.0 %collective-permute-start = (bf16[64,1152]{1,0:T(8,128)(2,1)}, bf16[64,1152]{1,0:T(8,128)(2,1)}, u32[]{:S(2)}, u32[]{:S(2)}) collective-permute-start(bf16[64,1152]{1,0:T(8,128)(2,1)} %copy.34), channel_id=1, source_target_pairs={{0,8},{8,16},{16,24},{24,32},{32,40},{40,48},{48,56},{56,64},{64,7... | collective-permute-start | bytes 442376 | tf_op jit(solution)/shard_map/while/body/eval_jaxpr/ppermute | solution.py:11
  246.1 11.1 %collective-permute-start = (bf16[64,1152]{1,0:T(8,128)(2,1)}, bf16[64,1152]{1,0:T(8,128)(2,1)}, u32[]{:S(2)}, u32[]{:S(2)}) collective-permute-start(bf16[64,1152]{1,0:T(8,128)(2,1)} %copy.34), channel_id=1, source_target_pairs={{0,8},{8,16},{16,24},{24,32},{32,40},{40,48},{48,56},{56,64},{64,7... | collective-permute-start | bytes 442376 | tf_op jit(solution)/shard_map/while/body/eval_jaxpr/ppermute | solution.py:11
  262.5 11.0 %collective-permute-start = (bf16[64,1152]{1,0:T(8,128)(2,1)}, bf16[64,1152]{1,0:T(8,128)(2,1)}, u32[]{:S(2)}, u32[]{:S(2)}) collective-permute-start(bf16[64,1152]{1,0:T(8,128)(2,1)} %copy.34), channel_id=1, source_target_pairs={{0,8},{8,16},{16,24},{24,32},{32,40},{40,48},{48,56},{56,64},{64,7... | collective-permute-start | bytes 442376 | tf_op jit(solution)/shard_map/while/body/eval_jaxpr/ppermute | solution.py:11
  278.9 11.0 %collective-permute-start = (bf16[64,1152]{1,0:T(8,128)(2,1)}, bf16[64,1152]{1,0:T(8,128)(2,1)}, u32[]{:S(2)}, u32[]{:S(2)}) collective-permute-start(bf16[64,1152]{1,0:T(8,128)(2,1)} %copy.34), channel_id=1, source_target_pairs={{0,8},{8,16},{16,24},{24,32},{32,40},{40,48},{48,56},{56,64},{64,7... | collective-permute-start | bytes 442376 | tf_op jit(solution)/shard_map/while/body/eval_jaxpr/ppermute | solution.py:11
  295.2 11.1 %collective-permute-start = (bf16[64,1152]{1,0:T(8,128)(2,1)}, bf16[64,1152]{1,0:T(8,128)(2,1)}, u32[]{:S(2)}, u32[]{:S(2)}) collective-permute-start(bf16[64,1152]{1,0:T(8,128)(2,1)} %copy.34), channel_id=1, source_target_pairs={{0,8},{8,16},{16,24},{24,32},{32,40},{40,48},{48,56},{56,64},{64,7... | collective-permute-start | bytes 442376 | tf_op jit(solution)/shard_map/while/body/eval_jaxpr/ppermute | solution.py:11
  311.6 11.0 %collective-permute-start = (bf16[64,1152]{1,0:T(8,128)(2,1)}, bf16[64,1152]{1,0:T(8,128)(2,1)}, u32[]{:S(2)}, u32[]{:S(2)}) collective-permute-start(bf16[64,1152]{1,0:T(8,128)(2,1)} %copy.34), channel_id=1, source_target_pairs={{0,8},{8,16},{16,24},{24,32},{32,40},{40,48},{48,56},{56,64},{64,7... | collective-permute-start | bytes 442376 | tf_op jit(solution)/shard_map/while/body/eval_jaxpr/ppermute | solution.py:11
  328.0 11.0 %collective-permute-start = (bf16[64,1152]{1,0:T(8,128)(2,1)}, bf16[64,1152]{1,0:T(8,128)(2,1)}, u32[]{:S(2)}, u32[]{:S(2)}) collective-permute-start(bf16[64,1152]{1,0:T(8,128)(2,1)} %copy.34), channel_id=1, source_target_pairs={{0,8},{8,16},{16,24},{24,32},{32,40},{40,48},{48,56},{56,64},{64,7... | collective-permute-start | bytes 442376 | tf_op jit(solution)/shard_map/while/body/eval_jaxpr/ppermute | solution.py:11
  344.3 11.1 %collective-permute-start = (bf16[64,1152]{1,0:T(8,128)(2,1)}, bf16[64,1152]{1,0:T(8,128)(2,1)}, u32[]{:S(2)}, u32[]{:S(2)}) collective-permute-start(bf16[64,1152]{1,0:T(8,128)(2,1)} %copy.34), channel_id=1, source_target_pairs={{0,8},{8,16},{16,24},{24,32},{32,40},{40,48},{48,56},{56,64},{64,7... | collective-permute-start | bytes 442376 | tf_op jit(solution)/shard_map/while/body/eval_jaxpr/ppermute | solution.py:11
  360.7 11.0 %collective-permute-start = (bf16[64,1152]{1,0:T(8,128)(2,1)}, bf16[64,1152]{1,0:T(8,128)(2,1)}, u32[]{:S(2)}, u32[]{:S(2)}) collective-permute-start(bf16[64,1152]{1,0:T(8,128)(2,1)} %copy.34), channel_id=1, source_target_pairs={{0,8},{8,16},{16,24},{24,32},{32,40},{40,48},{48,56},{56,64},{64,7... | collective-permute-start | bytes 442376 | tf_op jit(solution)/shard_map/while/body/eval_jaxpr/ppermute | solution.py:11
  377.1 11.0 %collective-permute-start = (bf16[64,1152]{1,0:T(8,128)(2,1)}, bf16[64,1152]{1,0:T(8,128)(2,1)}, u32[]{:S(2)}, u32[]{:S(2)}) collective-permute-start(bf16[64,1152]{1,0:T(8,128)(2,1)} %copy.34), channel_id=1, source_target_pairs={{0,8},{8,16},{16,24},{24,32},{32,40},{40,48},{48,56},{56,64},{64,7... | collective-permute-start | bytes 442376 | tf_op jit(solution)/shard_map/while/body/eval_jaxpr/ppermute | solution.py:11
  393.4 11.1 %collective-permute-start = (bf16[64,1152]{1,0:T(8,128)(2,1)}, bf16[64,1152]{1,0:T(8,128)(2,1)}, u32[]{:S(2)}, u32[]{:S(2)}) collective-permute-start(bf16[64,1152]{1,0:T(8,128)(2,1)} %copy.34), channel_id=1, source_target_pairs={{0,8},{8,16},{16,24},{24,32},{32,40},{40,48},{48,56},{56,64},{64,7... | collective-permute-start | bytes 442376 | tf_op jit(solution)/shard_map/while/body/eval_jaxpr/ppermute | solution.py:11
  409.8 11.0 %collective-permute-start = (bf16[64,1152]{1,0:T(8,128)(2,1)}, bf16[64,1152]{1,0:T(8,128)(2,1)}, u32[]{:S(2)}, u32[]{:S(2)}) collective-permute-start(bf16[64,1152]{1,0:T(8,128)(2,1)} %copy.34), channel_id=1, source_target_pairs={{0,8},{8,16},{16,24},{24,32},{32,40},{40,48},{48,56},{56,64},{64,7... | collective-permute-start | bytes 442376 | tf_op jit(solution)/shard_map/while/body/eval_jaxpr/ppermute | solution.py:11
  426.1 11.0 %collective-permute-start = (bf16[64,1152]{1,0:T(8,128)(2,1)}, bf16[64,1152]{1,0:T(8,128)(2,1)}, u32[]{:S(2)}, u32[]{:S(2)}) collective-permute-start(bf16[64,1152]{1,0:T(8,128)(2,1)} %copy.34), channel_id=1, source_target_pairs={{0,8},{8,16},{16,24},{24,32},{32,40},{40,48},{48,56},{56,64},{64,7... | collective-permute-start | bytes 442376 | tf_op jit(solution)/shard_map/while/body/eval_jaxpr/ppermute | solution.py:11
  442.5 11.1 %collective-permute-start = (bf16[64,1152]{1,0:T(8,128)(2,1)}, bf16[64,1152]{1,0:T(8,128)(2,1)}, u32[]{:S(2)}, u32[]{:S(2)}) collective-permute-start(bf16[64,1152]{1,0:T(8,128)(2,1)} %copy.34), channel_id=1, source_target_pairs={{0,8},{8,16},{16,24},{24,32},{32,40},{40,48},{48,56},{56,64},{64,7... | collective-permute-start | bytes 442376 | tf_op jit(solution)/shard_map/while/body/eval_jaxpr/ppermute | solution.py:11
  475.2 11.0 %collective-permute-start = (bf16[64,1152]{1,0:T(8,128)(2,1)}, bf16[64,1152]{1,0:T(8,128)(2,1)}, u32[]{:S(2)}, u32[]{:S(2)}) collective-permute-start(bf16[64,1152]{1,0:T(8,128)(2,1)} %copy.34), channel_id=1, source_target_pairs={{0,8},{8,16},{16,24},{24,32},{32,40},{40,48},{48,56},{56,64},{64,7... | collective-permute-start | bytes 442376 | tf_op jit(solution)/shard_map/while/body/eval_jaxpr/ppermute | solution.py:11
  491.6 11.1 %collective-permute-start = (bf16[64,1152]{1,0:T(8,128)(2,1)}, bf16[64,1152]{1,0:T(8,128)(2,1)}, u32[]{:S(2)}, u32[]{:S(2)}) collective-permute-start(bf16[64,1152]{1,0:T(8,128)(2,1)} %copy.34), channel_id=1, source_target_pairs={{0,8},{8,16},{16,24},{24,32},{32,40},{40,48},{48,56},{56,64},{64,7... | collective-permute-start | bytes 442376 | tf_op jit(solution)/shard_map/while/body/eval_jaxpr/ppermute | solution.py:11
  524.3 11.0 %collective-permute-start = (bf16[64,1152]{1,0:T(8,128)(2,1)}, bf16[64,1152]{1,0:T(8,128)(2,1)}, u32[]{:S(2)}, u32[]{:S(2)}) collective-permute-start(bf16[64,1152]{1,0:T(8,128)(2,1)} %copy.34), channel_id=1, source_target_pairs={{0,8},{8,16},{16,24},{24,32},{32,40},{40,48},{48,56},{56,64},{64,7... | collective-permute-start | bytes 442376 | tf_op jit(solution)/shard_map/while/body/eval_jaxpr/ppermute | solution.py:11
  540.7 11.1 %collective-permute-start = (bf16[64,1152]{1,0:T(8,128)(2,1)}, bf16[64,1152]{1,0:T(8,128)(2,1)}, u32[]{:S(2)}, u32[]{:S(2)}) collective-permute-start(bf16[64,1152]{1,0:T(8,128)(2,1)} %copy.34), channel_id=1, source_target_pairs={{0,8},{8,16},{16,24},{24,32},{32,40},{40,48},{48,56},{56,64},{64,7... | collective-permute-start | bytes 442376 | tf_op jit(solution)/shard_map/while/body/eval_jaxpr/ppermute | solution.py:11
  573.4 11.0 %collective-permute-start = (bf16[64,1152]{1,0:T(8,128)(2,1)}, bf16[64,1152]{1,0:T(8,128)(2,1)}, u32[]{:S(2)}, u32[]{:S(2)}) collective-permute-start(bf16[64,1152]{1,0:T(8,128)(2,1)} %copy.34), channel_id=1, source_target_pairs={{0,8},{8,16},{16,24},{24,32},{32,40},{40,48},{48,56},{56,64},{64,7... | collective-permute-start | bytes 442376 | tf_op jit(solution)/shard_map/while/body/eval_jaxpr/ppermute | solution.py:11
  589.8 11.1 %collective-permute-start = (bf16[64,1152]{1,0:T(8,128)(2,1)}, bf16[64,1152]{1,0:T(8,128)(2,1)}, u32[]{:S(2)}, u32[]{:S(2)}) collective-permute-start(bf16[64,1152]{1,0:T(8,128)(2,1)} %copy.34), channel_id=1, source_target_pairs={{0,8},{8,16},{16,24},{24,32},{32,40},{40,48},{48,56},{56,64},{64,7... | collective-permute-start | bytes 442376 | tf_op jit(solution)/shard_map/while/body/eval_jaxpr/ppermute | solution.py:11
  611.3 121.4 %all-to-all-start.1 = ((f32[8,144,64]{1,2,0:T(8,128)}), f32[8,144,64]{1,2,0:T(8,128)S(1)}, u32[]{:S(2)}, u32[]{:S(2)}) async-start(f32[8,144,64]{1,2,0:T(8,128)} %copy.24), calls=%async_computation.1 | async-start | bytes 1048576 | tf_op jit(solution)/shard_map/all_to_all | solution.py:82
  (74 other events, 520.1 us)
Sparse Core Ops, SparseCore 0:
  10.6 63.3 all-gather.1
  606.8 118.7 all-reduce.1
where the time goes:
time: 754 us; the launch traced here: 748 us
  matrix products  269 us (36%)
  waiting for transfers between devices  175 us (23%)
  blocking collectives  115 us (15%)
  local copies, waits for them, and re-layouts  82.8 us (11%)
  other arithmetic  52.1 us (7%)
  loops' own time  22 us (3%)
  between operations  20.2 us (3%)
  starting transfers between devices  11.6 us (2%)
    ppermute x64, waiting for transfers between devices, passed_along(): lax.ppermute(value, axis, [(i, (i + by) % size) for i in range(size)])  118 us
    psum x1, blocking collectives, per_device(): sums_all = lax.psum(totals, ('blk', 'col'))  115 us
    dot_general x32, matrix products, tile_terms(): lax.dot_general(weighted, text_block, (((0,), (0,)), ((), ())), preferred...  92 us
    dot_general x32, matrix products, tile_terms(): lax.dot_general(text_block, image_low, (((1,), (1,)), ((), ())), preferre...  90.7 us
    dot_general x32, matrix products, tile_terms(): text_part = jnp.dot(weighted, image_low, preferred_element_type=jnp.float32)  86.4 us
    while x96, local copies, waits for them, and re-layouts  71.7 us
    all_gather x1, waiting for transfers between devices, per_device(): image_rows = lax.all_gather(images, 'col', axis=0, tiled=True).T  45.1 us
    add x32, other arithmetic, turn(): return (text_block, text_grads, image_grads + image_part, totals + sums)  40.8 us
  transfers between devices with their start and end apart: 68, of which 34 were waited for; matrix products, arithmetic and copies ran while one was open for 43% of the time, Pallas kernels for 0%

commit v1 on v0

v1 whole, which is shorter than its diff:
```python
import jax
import jax.numpy as jnp
from jax import lax
from jax.sharding import PartitionSpec as P

epsilon = 1e-06
CONTRACT_ROWS = (((0,), (0,)), ((), ()))
CONTRACT_LANES = (((1,), (1,)), ((), ()))


def per_device(images, texts, log_temp, bias):
    own_index = lax.axis_index("blk")
    col_index = lax.axis_index("col")
    blocks = lax.axis_size("blk")
    cols = lax.axis_size("col")
    pairs_here = images.shape[1]
    both = jnp.stack([images, texts])
    norms = lax.psum(jnp.sum(both * both, axis=1), "col")
    scales = lax.rsqrt(norms + epsilon)[:, None, :]
    units = both * scales
    low = units.astype(jnp.bfloat16)
    image_low = lax.all_gather(low[0], "col", axis=0, tiled=True)
    text_low = lax.all_to_all(low[1], "col", split_axis=1, concat_axis=0, tiled=True)
    text_low = lax.all_gather(text_low, "blk", axis=1, tiled=True)
    temper = jnp.exp(log_temp[0])
    bias_value = bias[0]
    share = pairs_here // cols
    text_count = text_low.shape[1]
    scores = lax.dot_general(text_low, image_low, CONTRACT_ROWS, preferred_element_type=jnp.float32)
    order = jnp.arange(text_count, dtype=jnp.int32)
    text_pos = (order // share) * pairs_here + col_index * share + order % share
    image_pos = own_index * pairs_here + jnp.arange(pairs_here, dtype=jnp.int32)
    labels = jnp.where(text_pos[:, None] == image_pos[None, :], 1.0, -1.0).astype(jnp.float32)
    logits = temper * scores + bias_value
    losses = jax.nn.softplus(-labels * logits)
    slopes = -labels * jax.nn.sigmoid(-labels * logits)
    weighted = (temper * slopes).astype(jnp.bfloat16)
    sums = jnp.stack([jnp.sum(losses), jnp.sum(slopes * scores) * temper, jnp.sum(slopes)])
    image_part = jnp.dot(text_low, weighted, preferred_element_type=jnp.float32)
    text_part = lax.dot_general(image_low, weighted, CONTRACT_LANES, preferred_element_type=jnp.float32)
    image_grad = lax.psum_scatter(image_part, "col", scatter_dimension=0, tiled=True)
    text_grad = lax.psum_scatter(text_part, "blk", scatter_dimension=1, tiled=True)
    text_grad = lax.all_to_all(text_grad, "col", split_axis=0, concat_axis=1, tiled=True)
    grads = jnp.stack([image_grad, text_grad])
    dots = lax.psum(jnp.sum(units * grads, axis=1), "col")[:, None, :]
    grads = scales * (grads - units * dots)
    sums_all = lax.psum(sums, ("blk", "col"))
    total_rows = jnp.float32(pairs_here * blocks)
    pairs = total_rows * total_rows
    loss = jnp.reshape(sums_all[0] / pairs, (1,))
    grad_log_temp = jnp.reshape(sums_all[1] / pairs, (1,))
    grad_bias = jnp.reshape(sums_all[2] / pairs, (1,))
    return (loss, grads[0], grads[1], grad_log_temp, grad_bias)


def solution(mesh):
    in_specs = (P("col", "blk"), P("col", "blk"), P(), P())
    out_specs = (P(), P("col", "blk"), P("col", "blk"), P(), P())
    return jax.shard_map(
        per_device, mesh=mesh, in_specs=in_specs, out_specs=out_specs, check_vma=False
    )
```

time: 754 us -> 428 us (0.57)
  matrix products: 269 us -> 24.8 us
  local copies, waits for them, and re-layouts: 82.8 us -> 7.69 us
  waiting for transfers between devices: 175 us -> 228 us
  other arithmetic: 52.1 us -> 5.81 us
  loops' own time: 22 us -> 0 us
  blocking collectives: 115 us -> 133 us
    dot_general x96 -> x3, matrix products: 269 us -> 24.8 us  [the longest x1 9.89 us: per_device(): lax.dot_general(text_low, image_low, CONTRACT_ROWS, preferred_element_typ...]
    reduce_scatter x0 -> x2, waiting for transfers between devices: none -> 122 us  [the longest x1 122 us: per_device(): lax.psum_scatter(text_part, 'blk', scatter_dimension=1, tiled=True)]
    ppermute x64 -> x0, waiting for transfers between devices: 118 us -> none  [passed_along(): lax.ppermute(value, axis, [(i, (i + by) % size) for i in range(size)])]
    while x97 -> x0, local copies, waits for them, and re-layouts: 73.8 us -> none
    all_gather x1 -> x2, waiting for transfers between devices: 45.1 us -> 106 us  [the longest x1 69.3 us: per_device(): text_low = lax.all_gather(text_low, 'blk', axis=1, tiled=True)]
    add x96 -> x2, other arithmetic: 41 us -> 0.01 us  [the longest x1 0.01 us: per_device(): text_pos = order // share * pairs_here + col_index * share + order % share]
    another operation x1 -> x0, loops' own time: 22 us -> none  [per_device(): lax.fori_loop(0, cycle_size, turn, start)]
    all_to_all x0 -> x1, blocking collectives: none -> 11.2 us  [per_device(): lax.all_to_all(low[1], 'col', split_axis=1, concat_axis=0, tiled=True)]
  transfers between devices with their start and end apart: 68 -> 5, of which waited for: 34 -> 3; matrix products, arithmetic and copies ran while one was open for 43% -> 3% of each run, Pallas kernels for 0% -> 0%
where the time goes in v1:
time: 428 us; the launch traced here: 427 us
  waiting for transfers between devices  228 us (53%)
  blocking collectives  133 us (31%)
  matrix products  24.8 us (6%)
  between operations  21.2 us (5%)
  local copies, waits for them, and re-layouts  7.69 us (2%)
  starting transfers between devices  6.63 us (2%)
  other arithmetic  5.81 us (1%)
    reduce_scatter x1, waiting for transfers between devices, per_device(): lax.psum_scatter(text_part, 'blk', scatter_dimension=1, tiled=True)  122 us
    psum x1, blocking collectives, per_device(): sums_all = lax.psum(sums, ('blk', 'col'))  76.6 us
    all_gather x1, waiting for transfers between devices, per_device(): text_low = lax.all_gather(text_low, 'blk', axis=1, tiled=True)  69.3 us
    all_gather x1, waiting for transfers between devices, per_device(): image_low = lax.all_gather(low[0], 'col', axis=0, tiled=True)  36.3 us
    psum x1, blocking collectives, per_device(): norms = lax.psum(jnp.sum(both * both, axis=1), 'col')  23.6 us
    psum x1, blocking collectives, per_device(): dots = lax.psum(jnp.sum(units * grads, axis=1), 'col')[:, None, :]  22.1 us
    all_to_all x1, blocking collectives, per_device(): lax.all_to_all(low[1], 'col', split_axis=1, concat_axis=0, tiled=True)  11.2 us
    dot_general x1, matrix products, per_device(): lax.dot_general(text_low, image_low, CONTRACT_ROWS, preferred_element_typ...  9.89 us
  transfers between devices with their start and end apart: 5, of which 3 were waited for; matrix products, arithmetic and copies ran while one was open for 3% of the time, Pallas kernels for 0%

profile of v1, /device:TPU:2, one launch (start us, length us, event | category | flops | bytes accessed | tf_op | source)
XLA Modules:
  0.0 427.4 jit_solution(10787305120979484056)
XLA Ops:
  7.2 0.0 all-gather.6.cloned.1.call-start
  7.2 1.1 multiply_reduce_fusion.2
  8.3 23.6 %psum.21 = f32[2,512]{1,0:T(2,128)S(1)} all-reduce(f32[2,512]{1,0:T(2,128)S(1)} %multiply_reduce_fusion.2), channel_id=1, replica_groups=mesh['blk'=32,'col'=8] {'col'}, use_global_device_ids=true, to_apply=%region_1.0 | all-reduce | flops 1024 | bytes 8192 | tf_op jit(solution)/shard_map/psum | solution.py:18
  32.0 1.1 multiply_convert_fusion.3
  33.1 0.7 fusion.17
  33.8 0.0 all-gather.6.cloned.1.call-update
  33.8 0.0 all-gather.4.cloned.1.call-start
  33.8 0.1 copy.16
  34.0 11.2 %all_to_all.35 = bf16[144,8,64]{0,2,1:T(8,128)(2,1)S(1)} all-to-all(bf16[144,8,64]{0,2,1:T(8,128)(2,1)S(1)} %bitcast.44), channel_id=1, replica_groups=mesh['blk'=32,'col'=8] {'col'}, dimensions={1} | all-to-all | bytes 294912 | tf_op jit(solution)/shard_map/all_to_all | solution.py:23
  45.2 0.1 copy.13
  45.3 0.9 all_to_all.29
  46.3 0.0 reduce-scatter.5.cloned.1.call-start
  47.7 36.3 %all-gather.6.cloned.1.call-done = bf16[1,1152,512]{2,1,0:T(8,128)(2,1)} async-done(((bf16[1,144,512]{2,1,0:T(8,128)(2,1)}), bf16[1,1152,512]{2,1,0:T(8,128)(2,1)}) %all-gather.6.cloned.1.call-update) | async-done | bytes 1179664 | tf_op jit(solution)/shard_map/all_gather | solution.py:22
  84.0 69.3 %all-gather.4.cloned.1.call-done = bf16[1152,2048]{0,1:T(8,128)(2,1)} async-done(((bf16[1152,64]{0,1:T(8,128)(2,1)}), bf16[1152,2048]{0,1:T(8,128)(2,1)}) %all-gather.4.cloned.1.call-update) | async-done | bytes 4718608 | tf_op jit(solution)/shard_map/all_gather | solution.py:24
  153.4 9.9 %fusion = (f32[]{:T(128)}, f32[]{:T(128)}, f32[]{:T(128)}, f32[2048,512]{1,0:T(8,128)S(1)}) fusion(f32[]{:T(128)} %bitcast.31, f32[]{:T(128)} %bitcast, s32[512]{0:T(512)S(1)} %iota_add_fusion, s32[2048]{0:T(1024)S(1)} %fusion.14, bf16[1152,2048]{0,1:T(8,128)(2,1)} %all-gather.4.cloned.1.call-done, bf16[1,1152,512]{2,1,0:T(8,128)(2,1)} %all-gather.6.cloned.1.call-done), kind=kOutput, calls=%fused_computation.1 | convolution fusion | flops 2436890624 | bytes 10102804 | tf_op jit(solution)/shard_map/dot_general | solution.py:29
  163.3 1.9 copy-done.3
  165.2 6.7 %fusion.1 = f32[1152,2048]{0,1:T(8,128)} fusion(bf16[1,1152,512]{2,1,0:T(8,128)(2,1)S(1)} %copy-done.2, f32[]{:T(128)} %bitcast, f32[2048,512]{1,0:T(8,128)S(1)} %get-tuple-element.15, f32[]{:T(128)} %bitcast.32, s32[512]{0:T(512)S(1)} %iota_add_fusion, s32[2048]{0:T(1024)S(1)} %fusion.14), kind=kOutput, calls=%fused_computation.7 | convolution fusion | flops 2428502016 | bytes 14821384 | tf_op jit(solution)/shard_map/dot_general | solution.py:40
  171.9 0.0 reduce-scatter.5.cloned.1.call-update
  171.9 0.0 reduce-scatter.3.cloned.1.call-start
  172.0 8.3 %fusion.5 = f32[1152,512]{1,0:T(8,128)} fusion(bf16[1152,2048]{0,1:T(8,128)(2,1)} %all-gather.4.cloned.1.call-done, f32[]{:T(128)} %bitcast, f32[2048,512]{1,0:T(8,128)} %copy-done.3, f32[]{:T(128)} %bitcast.30, s32[512]{0:T(512)S(1)} %iota_add_fusion, s32[2048]{0:T(1024)S(1)} %fusion.14), kind=kOutput, calls=%fused_computation.11 | convolution fusion | flops 2428502016 | bytes 11282440 | tf_op jit(solution)/shard_map/dot_general | solution.py:39
  180.3 122.1 %reduce-scatter.5.cloned.1.call-done = f32[1152,64]{0,1:T(8,128)} async-done(((f32[1152,2048]{0,1:T(8,128)}), f32[1152,64]{0,1:T(8,128)}) %reduce-scatter.5.cloned.1.call-update) | async-done | bytes 294928 | tf_op jit(solution)/shard_map/reduce_scatter | solution.py:42
  302.3 1.3 all_to_all.30
  303.6 1.0 copy.14
  304.6 6.5 %all-to-all-start.1 = ((f32[8,144,64]{1,2,0:T(8,128)}), f32[8,144,64]{1,2,0:T(8,128)S(1)}, u32[]{:S(2)}, u32[]{:S(2)}) async-start(f32[8,144,64]{1,2,0:T(8,128)} %copy.14), calls=%async_computation.3 | async-start | bytes 1048576 | tf_op jit(solution)/shard_map/all_to_all | solution.py:43
  311.7 1.4 pad_maximum_fusion.2
  313.1 76.6 %psum.22 = f32[3]{0:T(128)S(1)} all-reduce(f32[3]{0:T(128)S(1)} %pad_maximum_fusion.2), channel_id=1, replica_groups=mesh['blk'=32,'col'=8] {'blk','col'}, use_global_device_ids=true, to_apply=%region_5.6 | all-reduce | flops 3 | bytes 24 | tf_op jit(solution)/shard_map/psum | solution.py:47
  389.6 0.6 fusion.18
  392.2 0.2 copy.17
  392.4 1.1 multiply_reduce_fusion.1
  393.5 22.1 %psum.23 = f32[2,512]{1,0:T(2,128)S(1)} all-reduce(f32[2,512]{1,0:T(2,128)S(1)} %multiply_reduce_fusion.1), channel_id=1, replica_groups=mesh['blk'=32,'col'=8] {'col'}, use_global_device_ids=true, to_apply=%region_9.10 | all-reduce | flops 1024 | bytes 8192 | tf_op jit(solution)/shard_map/psum | solution.py:45
  415.5 1.1 subtract_multiply_fusion
  416.6 0.8 slice_bitcast_fusion
  (14 shorter events, 0.1 us)
Async XLA Ops:
  7.2 76.9 %all-gather.6.cloned.1.call-start = ((), (), s32[]{:S(2)}) async-start(), calls=%async_computation.7 | async-start | bytes 1327104 | tf_op jit(solution)/shard_map/all_gather | solution.py:22
  33.8 119.6 %all-gather.4.cloned.1.call-start = ((), (), s32[]{:S(2)}) async-start(), calls=%async_computation.4 | async-start | bytes 4866048 | tf_op jit(solution)/shard_map/all_gather | solution.py:24
  46.3 256.0 %reduce-scatter.5.cloned.1.call-start = ((), (), s32[]{:S(2)}) async-start(), calls=%async_computation.6 | async-start | bytes 9732096 | tf_op jit(solution)/shard_map/reduce_scatter | solution.py:42
  153.4 11.8 %copy-start.2 = (bf16[1,1152,512]{2,1,0:T(8,128)(2,1)S(1)}, bf16[1,1152,512]{2,1,0:T(8,128)(2,1)}, u32[]{:S(2)}) copy-start(bf16[1,1152,512]{2,1,0:T(8,128)(2,1)} %all-gather.6.cloned.1.call-done) | copy-start | bytes 3538948
  163.3 1.9 copy-start.3
  171.9 220.4 %reduce-scatter.3.cloned.1.call-start = ((), (), s32[]{:S(2)}) async-start(), calls=%async_computation.5 | async-start | bytes 2654208 | tf_op jit(solution)/shard_map/reduce_scatter | solution.py:41
  180.2 212.1 %copy-start = (f32[144,512]{1,0:T(8,128)S(1)}, f32[144,512]{1,0:T(8,128)}, u32[]{:S(2)}) copy-start(f32[144,512]{1,0:T(8,128)} %param.5) | copy-start | bytes 884740
  180.2 212.1 %copy-start.1 = (f32[144,512]{1,0:T(8,128)S(1)}, f32[144,512]{1,0:T(8,128)}, u32[]{:S(2)}) copy-start(f32[144,512]{1,0:T(8,128)} %param.4) | copy-start | bytes 884740
  304.6 87.6 %all-to-all-start.1 = ((f32[8,144,64]{1,2,0:T(8,128)}), f32[8,144,64]{1,2,0:T(8,128)S(1)}, u32[]{:S(2)}, u32[]{:S(2)}) async-start(f32[8,144,64]{1,2,0:T(8,128)} %copy.14), calls=%async_computation.3 | async-start | bytes 1048576 | tf_op jit(solution)/shard_map/all_to_all | solution.py:43
Sparse Core Ops, SparseCore 0:
  33.9 50.0 all-gather.5
  86.5 66.8 all-gather.3
  172.0 130.2 reduce-scatter.4
  306.2 77.5 reduce-scatter.2

commit v2 on v1

v2 whole, which is shorter than its diff:
```python
import functools

import jax
import jax.numpy as jnp
from jax import lax
from jax.experimental import pallas as pl
from jax.experimental.pallas import tpu as pltpu
from jax.sharding import PartitionSpec as P

epsilon = 1e-06
F32 = jnp.float32
BF16 = jnp.bfloat16
MESH = pl.DeviceIdType.MESH
FEATURES = 1152
SHARE = 144
PAIRS = 512
DMA = pltpu.SemaphoreType.DMA


def device(x, y, z, core):
    return ((x % 2) * 16 + z * 2 + core, y * 2 + x // 2)


def hops(size, way, half):
    return size // 2 if (way == 0) == (half == 0) else size // 2 - 1


def step_of(way):
    return 1 if way == 0 else -1


class Gather:
    def __init__(self, piece, place, size, neighbour, sends, recvs):
        self.piece, self.place, self.size = piece, place, size
        self.neighbour, self.sends, self.recvs = neighbour, sends, recvs

    def copy(self, way, half, t, owner):
        ref = self.piece(owner, half)
        return pltpu.make_async_remote_copy(
            src_ref=ref, dst_ref=ref, send_sem=self.sends.at[way, half, t], recv_sem=self.recvs.at[way, half, t],
            device_id=self.neighbour[way], device_id_type=MESH,
        )

    def chains(self, t):
        return [(w, h) for h in (0, 1) for w in (0, 1) if t < hops(self.size, w, h)]

    def send(self, t):
        for way, half in self.chains(t):
            self.copy(way, half, t, (self.place - step_of(way) * t) % self.size).start()

    def arrive(self, t, then=None):
        for way, half in self.chains(t):
            owner = (self.place - step_of(way) * (t + 1)) % self.size
            self.copy(way, half, t, owner).wait_recv()
            if t + 1 < hops(self.size, way, half):
                self.copy(way, half, t + 1, owner).start()
            if then is not None:
                then(owner, half)

    def finish(self):
        for t in range(self.size // 2):
            for way, half in self.chains(t):
                self.copy(way, half, t, (self.place - step_of(way) * t) % self.size).wait_send()


class Scatter:
    def __init__(self, piece, place, size, neighbour, landed, sends, recvs):
        self.piece, self.place, self.size = piece, place, size
        self.neighbour, self.landed, self.sends, self.recvs = neighbour, landed, sends, recvs

    def copy(self, way, half, t):
        n = hops(self.size, way, half)
        if t == 0:
            src = self.piece((self.place + step_of(way) * n) % self.size, half)
        else:
            src = self.landed.at[way, half, t - 1]
        return pltpu.make_async_remote_copy(
            src_ref=src, dst_ref=self.landed.at[way, half, t], send_sem=self.sends.at[way, half, t],
            recv_sem=self.recvs.at[way, half, t], device_id=self.neighbour[way], device_id_type=MESH,
        )

    def chains(self, t):
        every = [(w, h) for h in (0, 1) for w in (0, 1)]
        every.sort(key=lambda c: -hops(self.size, *c))
        return [c for c in every if t < hops(self.size, *c)]

    def send(self):
        for way, half in self.chains(0):
            self.copy(way, half, 0).start()

    def arrive(self, t):
        for way, half in self.chains(t):
            n = hops(self.size, way, half)
            self.copy(way, half, t).wait_recv()
            own = self.piece((self.place + step_of(way) * (n - t - 1)) % self.size, half)
            slot = self.landed.at[way, half, t]
            if t + 1 < n:
                slot[...] = slot[...] + own[...]
                self.copy(way, half, t + 1).start()
            else:
                own[...] = own[...] + slot[...]

    def finish(self):
        for t in range(self.size // 2):
            for way, half in self.chains(t):
                self.copy(way, half, t).wait_send()


def kernel(
    im_ref, tx_ref, lt_ref, bias_ref,
    loss_ref, gi_ref, gt_ref, glt_ref, gb_ref,
    norm_buf, dot_buf, scale_buf, ts_buf, img, txt, txt_t, wgt, gia, gib, gt, sib_buf,
    land_a1, land_b1, land_a2, land_b2, land_z, sum_buf, tg,
    col_sems, a2a_sems, sib_sems, ga_sems, gb_sems, gz_sems, gy_sems, gx_sems,
    sa_sems, sb_sems, sa2_sems, sb2_sems, sz_sems, total_sems,
):
    b = lax.axis_index("blk")
    c = lax.axis_index("col")
    xlo, z, k = b // 16, (b // 2) % 8, b % 2
    y, xhi = c // 2, c % 2
    x = xhi * 2 + xlo
    fh = 1 - k
    sibling = device(x, y, z, 1 - k)
    x_near = [device((x + 1) % 4, y, z, k), device((x + 3) % 4, y, z, k)]
    y_near = [device(x, (y + 1) % 4, z, k), device(x, (y + 3) % 4, z, k)]
    z_near = [device(x, y, (z + 1) % 8, k), device(x, y, (z + 7) % 8, k)]
    x_other = device(xhi * 2 + 1 - xlo, y, z, k)
    col_peers = [(b, (c + i) % 8) for i in range(1, 8)]
    z_peers = [device(x, y, (z + i) % 8, k) for i in range(1, 8)]
    text_to = [(xlo * 16 + z * 2 + 1 - c // 4, 4 * k + s) for s in range(4)]
    text_from = [(xlo * 16 + z * 2 + c // 4, 4 * fh + i) for i in range(4)]

    barrier = pltpu.get_barrier_semaphore()
    greeted = [sibling] + x_near + col_peers + z_peers + text_to + text_from
    for peer in greeted:
        pl.semaphore_signal(barrier, inc=1, device_id=peer, device_id_type=MESH)

    def remote(src, dst, send_sem, recv_sem, peer):
        return pltpu.make_async_remote_copy(
            src_ref=src, dst_ref=dst, send_sem=send_sem, recv_sem=recv_sem, device_id=peer, device_id_type=MESH
        )

    im = im_ref[...]
    tx = tx_ref[...]
    norm_buf[c, 0:1, :] = jnp.sum(im * im, axis=0, keepdims=True)
    norm_buf[c, 1:2, :] = jnp.sum(tx * tx, axis=0, keepdims=True)
    pl.semaphore_wait(barrier, len(greeted))

    def over_col(buf, stage):
        def copies():
            return [
                remote(buf.at[c], buf.at[c], col_sems.at[stage, 0, i], col_sems.at[stage, 1, i], col_peers[i])
                for i in range(7)
            ]

        for copy in copies():
            copy.start()
        for i in range(7):
            src = buf.at[(c + 7 - i) % 8]
            remote(src, src, col_sems.at[stage, 0, i], col_sems.at[stage, 1, i], col_peers[i]).wait_recv()
        return copies

    norms_out = over_col(norm_buf, 0)
    norms = norm_buf[0]
    for i in range(1, 8):
        norms = norms + norm_buf[i]
    scale_buf[...] = lax.rsqrt(norms + epsilon)
    scale_i = scale_buf[0:1, :]
    scale_t = scale_buf[1:2, :]

    ts_buf[...] = (tx_ref[...] * scale_t).astype(BF16)
    own_cols = pl.ds(pl.multiple_of(z * 128, 128), 128)
    text_sends = []
    for s in range(4):
        copy = remote(
            ts_buf.at[:, pl.ds(s * 128, 128)],
            txt.at[pl.ds(pl.multiple_of(c * SHARE, 16), SHARE), own_cols],
            a2a_sems.at[0, 0, s], a2a_sems.at[0, 1, c % 4], text_to[s],
        )
        copy.start()
        text_sends.append(copy)
    im_low = (im_ref[...] * scale_i).astype(BF16)
    im_rows = pl.ds(pl.multiple_of(xhi * SHARE, 16), SHARE)
    im_cols = pl.ds(pl.multiple_of(xlo * 256, 256), 256)
    img[0, y, im_rows, im_cols] = im_low[:, 0:256]
    img[1, y, im_rows, im_cols] = im_low[:, 256:512]

    def rows_of(xx):
        return pl.ds(pl.multiple_of((xx // 2) * SHARE, 16), SHARE)

    def near_cols(xx, half):
        return pl.ds(pl.multiple_of((xx % 2) * 256 + half * 128, 128), 128)

    ga = Gather(lambda o, h: img.at[0, y, rows_of(o), near_cols(o, h)], x, 4, x_near, ga_sems.at[0], ga_sems.at[1])
    gb = Gather(lambda o, h: img.at[1, o, im_rows, near_cols(x, h)], y, 4, y_near, gb_sems.at[0], gb_sems.at[1])
    gy = Gather(lambda o, h: img.at[0, o, pl.ds(h * SHARE, SHARE), :], y, 4, y_near, gy_sems.at[0], gy_sems.at[1])
    gx = Gather(
        lambda o, h: img.at[1, pl.ds(h * 2, 2), rows_of(o), pl.ds(pl.multiple_of((o % 2) * 256, 256), 256)],
        x, 4, x_near, gx_sems.at[0], gx_sems.at[1],
    )

    def text_piece(o, h):
        return txt.at[pl.ds(pl.multiple_of(fh * 576 + h * 288, 16), 288), pl.ds(pl.multiple_of(o * 128, 128), 128)]

    gz = Gather(text_piece, z, 8, z_near, gz_sems.at[0], gz_sems.at[1])

    def to_sibling(o, h):
        ref = text_piece(o, h)
        remote(ref, ref, sib_sems.at[0], sib_sems.at[1], sibling).start()

    ga.send(0)
    gb.send(0)
    for i in range(4):
        ref = txt.at[pl.ds(pl.multiple_of(fh * 576 + i * SHARE, 16), SHARE), own_cols]
        remote(ref, ref, a2a_sems.at[0, 0, i], a2a_sems.at[0, 1, i], sibling).wait_recv()
    gz.send(0)
    to_sibling(z, 0)
    to_sibling(z, 1)
    ga.arrive(0)
    gb.arrive(0)
    ga.arrive(1)
    gy.send(0)
    gb.arrive(1)
    gx.send(0)
    gz.arrive(0, to_sibling)
    gz.arrive(1, to_sibling)
    gy.arrive(0)
    gx.arrive(0)
    gz.arrive(2, to_sibling)
    gz.arrive(3, to_sibling)
    theirs = txt.at[pl.ds(pl.multiple_of((1 - fh) * 576, 16), 576), :]
    mine = txt.at[pl.ds(pl.multiple_of(fh * 576, 16), 576), :]
    remote(mine, theirs, sib_sems.at[0], sib_sems.at[1], sibling).wait_recv()

    def turn(o, _):
        cols = pl.ds(pl.multiple_of(o * 128, 128), 128)
        txt_t[cols, :] = txt[:, cols].T
        return 0

    lax.fori_loop(0, 8, turn, 0)
    gy.arrive(1)
    gx.arrive(1)

    temper = jnp.exp(jnp.full((1, 256), lt_ref[0], F32))
    bias_value = bias_ref[0]
    sum_buf[0] = jnp.zeros((3, 8, 128), F32)

    def tile(i, _):
        h, n, m = i // 4, (i // 2) % 2, i % 2
        rows = pl.ds(pl.multiple_of(m * 512, 512), 512)
        cols = pl.ds(pl.multiple_of(n * 256, 256), 256)
        images = img[h, :, :, cols].reshape(FEATURES, 256)
        scores = jnp.dot(txt_t[rows, :], images, preferred_element_type=F32)
        j = lax.broadcasted_iota(jnp.int32, (512, 1), 0) + m * 512
        text_pos = (xlo * 16 + (j // 128) * 2 + c // 4) * PAIRS + (c % 4) * 128 + j % 128
        image_pos = (n * 16 + z * 2 + k) * PAIRS + h * 256 + lax.broadcasted_iota(jnp.int32, (1, 256), 1)
        same = text_pos == image_pos
        logits = temper * scores + bias_value
        u = jnp.where(same, -logits, logits)
        e = jnp.exp(-jnp.abs(u))
        r = 1.0 / (1.0 + e)
        sig = jnp.where(u >= 0, r, e * r)
        losses = jnp.maximum(u, 0.0) + jnp.log1p(e)
        slopes = jnp.where(same, -sig, sig)
        wgt[h, rows, cols] = (temper * slopes).astype(BF16)

        def fold(v):
            v = jnp.sum(v.reshape(64, 8, 256), axis=0)
            return v[:, 0:128] + v[:, 128:256]

        sum_buf[0, 0] += fold(losses)
        sum_buf[0, 1] += fold(slopes * scores)
        sum_buf[0, 2] += fold(slopes)
        return 0

    lax.fori_loop(0, 8, tile, 0)

    def total_stage(stage, base, peers, sources):
        copies = []
        for i, peer in enumerate(peers):
            copies.append(remote(
                sum_buf.at[base], sum_buf.at[base + 1 + i],
                total_sems.at[0, stage, i], total_sems.at[1, stage, i], peer,
            ))
        for copy in copies:
            copy.start()

        def done():
            for copy in copies:
                copy.wait()
            total = sum_buf[base]
            for i in range(len(peers)):
                total = total + sum_buf[base + 1 + i]
            sum_buf[base + 1 + len(peers)] = total

        return done

    s_sib = total_stage(0, 0, [sibling], None)

    def text_part(n, _):
        rows = pl.ds(pl.multiple_of(n * 256, 256), 256)
        contract = (((1,), (1,)), ((), ()))
        part = lax.dot_general(
            img[0].reshape(FEATURES, 512), wgt[0, rows, :], contract, preferred_element_type=F32
        ) + lax.dot_general(img[1].reshape(FEATURES, 512), wgt[1, rows, :], contract, preferred_element_type=F32)
        gt[2 * n] = part[:, 0:128]
        gt[2 * n + 1] = part[:, 128:256]
        return 0

    lax.fori_loop(0, 4, text_part, 0)
    grad_sib = remote(
        gt.at[:, pl.ds(pl.multiple_of((1 - fh) * 576, 8), 576), :], sib_buf, sib_sems.at[2], sib_sems.at[3], sibling
    )
    grad_sib.start()
    s_sib()
    s_x = total_stage(1, 2, [x_other], None)

    def image_part(h):
        def body(n, _):
            cols = pl.ds(pl.multiple_of(n * 256, 256), 256)
            part = jnp.dot(txt[...], wgt[h, :, cols], preferred_element_type=F32)
            for yy in range(4):
                for hi in range(2):
                    piece = part[yy * 288 + hi * SHARE : yy * 288 + hi * SHARE + SHARE, :]
                    if h == 0:
                        gia[yy, hi * 2 + n] = piece
                    else:
                        gib[hi * 2 + n, yy] = piece
            return 0

        lax.fori_loop(0, 2, body, 0)

    pair = lambda h: pl.ds(h * 2, 2)
    near = lambda h: pl.ds(h * 72, 72)
    sa = Scatter(lambda o, h: gia.at[o, pair(h)], y, 4, y_near, land_a1, sa_sems.at[0], sa_sems.at[1])
    sb = Scatter(lambda o, h: gib.at[o, pair(h)], x, 4, x_near, land_b1, sb_sems.at[0], sb_sems.at[1])
    sa2 = Scatter(lambda o, h: gia.at[y, o, near(h)], x, 4, x_near, land_a2, sa2_sems.at[0], sa2_sems.at[1])
    sb2 = Scatter(lambda o, h: gib.at[x, o, near(h)], y, 4, y_near, land_b2, sb2_sems.at[0], sb2_sems.at[1])
    gt_rows = lambda h: pl.ds(pl.multiple_of(fh * 576 + h * 288, 8), 288)
    sz = Scatter(lambda o, h: gt.at[o, gt_rows(h)], z, 8, z_near, land_z, sz_sems.at[0], sz_sems.at[1])

    image_part(0)
    sa.send()
    s_x()
    s_z = total_stage(2, 4, z_peers, None)
    grad_sib.wait()
    own_half = pl.ds(pl.multiple_of(fh * 576, 8), 576)

    def join(o, _):
        gt[o, own_half] = gt[o, own_half] + sib_buf[o]
        return 0

    lax.fori_loop(0, 8, join, 0)
    sz.send()
    image_part(1)
    sb.send()
    s_z()
    s_col = total_stage(3, 12, col_peers, None)
    sz.arrive(0)
    s_col()
    total = sum_buf[20]
    pairs_inv = 1.0 / float(16384 * 16384)
    loss_ref[0] = jnp.sum(total[0]) * pairs_inv
    glt_ref[0] = jnp.sum(total[1] * temper[:, 0:128]) * pairs_inv
    gb_ref[0] = jnp.sum(total[2]) * pairs_inv
    sz.arrive(1)
    sa.arrive(0)
    sb.arrive(0)
    sz.arrive(2)
    sa.arrive(1)
    sa2.send()
    sb.arrive(1)
    sb2.send()
    sz.arrive(3)

    back = []
    for i in range(4):
        copy = remote(
            gt.at[z, pl.ds(pl.multiple_of(fh * 576 + i * SHARE, 8), SHARE), :],
            tg.at[:, pl.ds(pl.multiple_of((c % 4) * 128, 128), 128)],
            a2a_sems.at[1, 0, i], a2a_sems.at[1, 1, c % 4], text_from[i],
        )
        copy.start()
        back.append(copy)
    sa2.arrive(0)
    sb2.arrive(0)
    sa2.arrive(1)
    sb2.arrive(1)
    grad_a = gia[y, x]
    grad_b = gib[x, y]
    unit_i = im_ref[...] * scale_buf[0:1, :]
    dot_buf[c, 0:1, 0:256] = jnp.sum(unit_i[:, 0:256] * grad_a, axis=0, keepdims=True)
    dot_buf[c, 0:1, 256:512] = jnp.sum(unit_i[:, 256:512] * grad_b, axis=0, keepdims=True)
    for s in range(4):
        ref = tg.at[:, pl.ds(s * 128, 128)]
        remote(ref, ref, a2a_sems.at[1, 0, s], a2a_sems.at[1, 1, s], sibling).wait_recv()
    unit_t = tx_ref[...] * scale_buf[1:2, :]
    dot_buf[c, 1:2, :] = jnp.sum(unit_t * tg[...], axis=0, keepdims=True)
    dots_out = over_col(dot_buf, 1)
    dots = dot_buf[0]
    for i in range(1, 8):
        dots = dots + dot_buf[i]
    scale_i = scale_buf[0:1, :]
    scale_t = scale_buf[1:2, :]
    unit_i = im_ref[...] * scale_i
    unit_t = tx_ref[...] * scale_t
    gi_ref[:, 0:256] = scale_i[:, 0:256] * (gia[y, x] - unit_i[:, 0:256] * dots[0:1, 0:256])
    gi_ref[:, 256:512] = scale_i[:, 256:512] * (gib[x, y] - unit_i[:, 256:512] * dots[0:1, 256:512])
    gt_ref[...] = scale_t * (tg[...] - unit_t * dots[1:2, :])

    for copies in (norms_out, dots_out):
        for copy in copies():
            copy.wait_send()
    for copy in text_sends + back:
        copy.wait_send()
    remote(mine, theirs, sib_sems.at[0], sib_sems.at[1], sibling).wait_send()
    for stage in (ga, gb, gy, gx, gz, sa, sb, sa2, sb2, sz):
        stage.finish()


def per_device(images, texts, log_temp, bias):
    vmem = pl.BlockSpec(memory_space=pltpu.VMEM)
    smem = pl.BlockSpec(memory_space=pltpu.SMEM)
    one = jax.ShapeDtypeStruct((1,), F32)
    grad = jax.ShapeDtypeStruct((SHARE, PAIRS), F32)
    scratch = [
        pltpu.VMEM((8, 8, PAIRS), F32),
        pltpu.VMEM((8, 8, PAIRS), F32),
        pltpu.VMEM((8, PAIRS), F32),
        pltpu.VMEM((SHARE, PAIRS), BF16),
        pltpu.VMEM((2, 4, 2 * SHARE, 512), BF16),
        pltpu.VMEM((FEATURES, 1024), BF16),
        pltpu.VMEM((1024, FEATURES), BF16),
        pltpu.VMEM((2, 1024, 512), BF16),
        pltpu.VMEM((4, 4, SHARE, 256), F32),
        pltpu.VMEM((4, 4, SHARE, 256), F32),
        pltpu.VMEM((8, FEATURES, 128), F32),
        pltpu.VMEM((8, 576, 128), F32),
        pltpu.VMEM((2, 2, 2, 2, SHARE, 256), F32),
        pltpu.VMEM((2, 2, 2, 2, SHARE, 256), F32),
        pltpu.VMEM((2, 2, 2, 72, 256), F32),
        pltpu.VMEM((2, 2, 2, 72, 256), F32),
        pltpu.VMEM((2, 2, 4, 288, 128), F32),
        pltpu.VMEM((21, 3, 8, 128), F32),
        pltpu.VMEM((SHARE, PAIRS), F32),
        DMA((2, 2, 7)),
        DMA((2, 2, 4)),
        DMA((4,)),
        DMA((2, 2, 2, 2)), DMA((2, 2, 2, 2)),
        DMA((2, 2, 2, 4)),
        DMA((2, 2, 2, 2)), DMA((2, 2, 2, 2)),
        DMA((2, 2, 2, 2)), DMA((2, 2, 2, 2)), DMA((2, 2, 2, 2)), DMA((2, 2, 2, 2)),
        DMA((2, 2, 2, 4)),
        DMA((2, 4, 7)),
    ]
    return pl.pallas_call(
        kernel,
        out_shape=(one, grad, grad, one, one),
        in_specs=[vmem, vmem, smem, smem],
        out_specs=(smem, vmem, vmem, smem, smem),
        scratch_shapes=scratch,
        compiler_params=pltpu.CompilerParams(
            collective_id=0, has_side_effects=True, vmem_limit_bytes=56 * 2**20
        ),
        name="contrastive",
    )(images, texts, log_temp, bias)


def solution(mesh):
    in_specs = (P("col", "blk"), P("col", "blk"), P(), P())
    out_specs = (P(), P("col", "blk"), P("col", "blk"), P(), P())
    return jax.shard_map(
        per_device, mesh=mesh, in_specs=in_specs, out_specs=out_specs, check_vma=False
    )
```

time: 428 us -> 116 us (0.27)
  waiting for transfers between devices: 228 us -> 0 us
  blocking collectives: 133 us -> 0 us
  Pallas kernels: 0 us -> 106 us
  matrix products: 24.8 us -> 0 us
  between operations: 21.2 us -> 7.19 us
  starting transfers between devices: 6.63 us -> 0 us
  other arithmetic: 5.81 us -> 0 us
  local copies, waits for them, and re-layouts: 7.69 us -> 2.46 us
    psum x3 -> x0, blocking collectives: 122 us -> none  [the longest x1 76.6 us: per_device(): sums_all = lax.psum(sums, ('blk', 'col'))]
    reduce_scatter x2 -> x0, waiting for transfers between devices: 122 us -> none  [the longest x1 122 us: per_device(): lax.psum_scatter(text_part, 'blk', scatter_dimension=1, tiled=True)]
    all_gather x2 -> x0, waiting for transfers between devices: 106 us -> none  [the longest x1 69.3 us: per_device(): text_low = lax.all_gather(text_low, 'blk', axis=1, tiled=True)]
    pallas_call x0 -> x1, Pallas kernels: none -> 106 us  [per_device(): pl.pallas_call(kernel, out_shape=(one, grad, grad, one, one), in_specs=[v...]
    dot_general x3 -> x0, matrix products: 24.8 us -> none  [the longest x1 9.89 us: per_device(): lax.dot_general(text_low, image_low, CONTRACT_ROWS, preferred_element_typ...]
    all_to_all x1 -> x0, blocking collectives: 11.2 us -> none  [per_device(): lax.all_to_all(low[1], 'col', split_axis=1, concat_axis=0, tiled=True)]
    all_to_all x1 -> x0, starting transfers between devices: 6.46 us -> none  [per_device(): lax.all_to_all(text_grad, 'col', split_axis=0, concat_axis=1, tiled=True)]
  transfers between devices with their start and end apart: 5 -> 0, of which waited for: 3 -> 0; matrix products, arithmetic and copies ran while one was open for 3% -> 0% of each run, Pallas kernels for 0% -> 0%
where the time goes in v2:
time: 116 us; the launch traced here: 115 us
  Pallas kernels  106 us (91%)
  between operations  7.19 us (6%)
  local copies, waits for them, and re-layouts  2.46 us (2%)
    pallas_call x1, Pallas kernels, per_device(): pl.pallas_call(kernel, out_shape=(one, grad, grad, one, one), in_specs=[v...  106 us
    unnamed x4, local copies, waits for them, and re-layouts  2.46 us

profile of v2, /device:TPU:2, one launch (start us, length us, event | category | flops | bytes accessed | tf_op | source)
XLA Modules:
  0.0 115.3 jit_solution(2963638099639511309)
XLA Ops:
  1.9 105.6 %contrastive.1 = (f32[1]{0:T(128)}, f32[144,512]{1,0:T(8,128)}, f32[144,512]{1,0:T(8,128)}, f32[1]{0:T(128)}, f32[1]{0:T(128)}) custom-call(f32[144,512]{1,0:T(8,128)} %im_ref.1, f32[144,512]{1,0:T(8,128)} %tx_ref.1, f32[1]{0:T(128)S(6)} %copy.14.lt_ref, f32[1]{0:T(128)S(6)} %copy.15.bias_ref), custom_call_target="tpu_custom_call" | custom-call | tf_op jit(solution)/shard_map/contrastive/pallas_call | solution.py:456
  108.2 0.0 copy-start
  108.2 1.7 %copy.17 = f32[144,512]{1,0:T(8,128)} copy(f32[144,512]{1,0:T(8,128)} %get-tuple-element.11) | data formatting | bytes 589824
  110.0 0.0 copy-done
  110.0 0.7 copy.18
Async XLA Ops:
  108.2 1.8 %copy-start = (f32[144,512]{1,0:T(8,128)S(1)}, f32[144,512]{1,0:T(8,128)}, u32[]{:S(2)}) copy-start(f32[144,512]{1,0:T(8,128)} %get-tuple-element.12) | copy-start | bytes 884740

commit v3 on v1

v3 whole, which is shorter than its diff:
```python
import functools

import jax
import jax.numpy as jnp
from jax import lax
from jax.experimental import pallas as pl
from jax.experimental.pallas import tpu as pltpu
from jax.sharding import PartitionSpec as P

epsilon = 1e-06
F32 = jnp.float32
BF16 = jnp.bfloat16
MESH = pl.DeviceIdType.MESH
FEATURES = 1152
NT = (((1,), (1,)), ((), ()))
SHARE = 144
PAIRS = 512
DMA = pltpu.SemaphoreType.DMA


def device(x, y, z, core):
    return ((x % 2) * 16 + z * 2 + core, y * 2 + x // 2)


class Ring:
    def __init__(self, piece, place, size, neighbour, chains, sends, recvs, landed=None):
        self.piece, self.place, self.size, self.neighbour = piece, place, size, neighbour
        self.sends, self.recvs, self.landed = sends, recvs, landed
        self.all = []
        base = 0
        for way, half, n in chains:
            self.all.append((way, half, n, base))
            base += n

    def at(self, offset):
        return (self.place + offset + 2 * self.size) % self.size

    def chains(self, t):
        return [chain for chain in self.all if t < chain[2]]

    def remote(self, chain, t, src, dst):
        way, _, _, base = chain
        return pltpu.make_async_remote_copy(
            src_ref=src, dst_ref=dst, send_sem=self.sends.at[base + t], recv_sem=self.recvs.at[base + t],
            device_id=self.neighbour[way], device_id_type=MESH,
        )

    def send(self, only=None):
        for chain in self.all:
            if only is None or chain[:2] in only:
                self.copy(chain, 0).start()

    def finish(self):
        for t in range(self.size):
            for chain in self.chains(t):
                self.copy(chain, t).wait_send()


class Gather(Ring):
    def copy(self, chain, t):
        way, half = chain[:2]
        ref = self.piece(self.at(-t if way == 0 else t), half)
        return self.remote(chain, t, ref, ref)

    def arrive(self, t, then=None, only=None):
        for chain in self.chains(t):
            way, half, n, base = chain
            if only is not None and chain[:2] not in only:
                continue
            owner = self.at(-t - 1 if way == 0 else t + 1)
            ref = self.piece(owner, half)
            self.remote(chain, t, ref, ref).wait_recv()
            if t + 1 < n:
                self.copy(chain, t + 1).start()
            if then is not None:
                then(owner, half, base + t)


class Scatter(Ring):
    def copy(self, chain, t):
        way, half, n, base = chain
        if t == 0:
            src = self.piece(self.at(n if way == 0 else -n), half)
        else:
            src = self.landed.at[base + t - 1]
        return self.remote(chain, t, src, self.landed.at[base + t])

    def arrive(self, t, only=None):
        for chain in self.chains(t):
            way, half, n, base = chain
            if only is not None and chain[:2] not in only:
                continue
            self.copy(chain, t).wait_recv()
            ahead = n - t - 1
            own = self.piece(self.at(ahead if way == 0 else -ahead), half)
            slot = self.landed.at[base + t]
            if ahead > 0:
                slot[...] = slot[...] + own[...]
                self.copy(chain, t + 1).start()
            else:
                own[...] = own[...] + slot[...]


class Direct:
    def __init__(self, piece, place, axis, sends, recvs, landed=None):
        self.piece, self.place, self.axis = piece, place, axis
        self.sends, self.recvs, self.landed = sends, recvs, landed

    def copy(self, i):
        if self.landed is None:
            src = dst = self.piece(self.place, 0)
        else:
            src, dst = self.piece((self.place + i + 1) % 4, 0), self.landed.at[i]
        return pltpu.make_async_remote_copy(
            src_ref=src, dst_ref=dst, send_sem=self.sends.at[i], recv_sem=self.recvs.at[i],
            device_id=self.axis(i + 1), device_id_type=MESH,
        )

    def send(self):
        for i in (1, 0, 2):
            self.copy(i).start()

    def arrive(self):
        for i in range(3):
            self.copy(i).wait_recv()
        if self.landed is not None:
            own = self.piece(self.place, 0)
            own[...] = own[...] + (self.landed[0] + self.landed[1] + self.landed[2])

    def finish(self):
        for i in range(3):
            self.copy(i).wait_send()


def finish_all(started):
    for finish in started:
        finish()


def kernel(
    im_ref, tx_ref, knob_ref,
    mean_ref, gi_ref, gt_ref,
    norm_buf, dot_buf, scale_buf, ts_buf, img, txt, txt_t, wgt, gi, gt, sib_buf,
    land_1, land_2, land_z, sum_buf, sum_z, tg,
    col_sems, a2a_sems, sib_sems, pair_sems, g_sems, gz_sems, s_sems, sz_sems, gs_sems, total_sems,
):
    b = lax.axis_index("blk")
    c = lax.axis_index("col")
    xlo, z, k = b // 16, (b // 2) % 8, b % 2
    y, xhi = c // 2, c % 2
    x = xhi * 2 + xlo
    fh = 1 - k
    sibling = device(x, y, z, 1 - k)
    x_near = [device((x + 1) % 4, y, z, k), device((x + 3) % 4, y, z, k)]
    y_near = [device(x, (y + 1) % 4, z, k), device(x, (y + 3) % 4, z, k)]
    on_x = lambda i: device((x + i) % 4, y, z, k)
    on_y = lambda i: device(x, (y + i) % 4, z, k)
    z_near = [device(x, y, (z + 1) % 8, k), device(x, y, (z + 7) % 8, k)]
    x_other = device(xhi * 2 + 1 - xlo, y, z, k)
    col_peers = [(b, (c + i) % 8) for i in range(1, 8)]
    across = [(xlo * 16 + z * 2 + 1 - k, 4 * (c // 4) + i) for i in range(4)]
    text_to = [(xlo * 16 + z * 2 + 1 - c // 4, 4 * k + s) for s in range(4)]
    text_from = [(xlo * 16 + z * 2 + c // 4, 4 * fh + i) for i in range(4)]
    started = []

    barrier = pltpu.get_barrier_semaphore()
    greeted = across + x_near + z_near + col_peers
    for peer in greeted:
        pl.semaphore_signal(barrier, inc=1, device_id=peer, device_id_type=MESH)

    def remote(src, dst, send_sem, recv_sem, peer):
        return pltpu.make_async_remote_copy(
            src_ref=src, dst_ref=dst, send_sem=send_sem, recv_sem=recv_sem, device_id=peer, device_id_type=MESH
        )

    im = im_ref[...]
    tx = tx_ref[...]
    norm_buf[c, 0:1, :] = jnp.sum(im * im, axis=0, keepdims=True)
    norm_buf[c, 1:2, :] = jnp.sum(tx * tx, axis=0, keepdims=True)
    pl.semaphore_wait(barrier, len(greeted))

    def over_col(buf, stage):
        sends = [
            remote(buf.at[c], buf.at[c], col_sems.at[stage, 0, i], col_sems.at[stage, 1, i], col_peers[i])
            for i in range(7)
        ]
        for copy in sends:
            copy.start()
        started.append(lambda: [copy.wait_send() for copy in sends])

        def total():
            for i in range(7):
                src = buf.at[(c + 7 - i) % 8]
                remote(src, src, col_sems.at[stage, 0, i], col_sems.at[stage, 1, i], col_peers[i]).wait_recv()
            whole = buf[0]
            for i in range(1, 8):
                whole = whole + buf[i]
            return whole

        return total

    scale_buf[...] = lax.rsqrt(over_col(norm_buf, 0)() + epsilon)
    scale_i = scale_buf[0:1, :]
    scale_t = scale_buf[1:2, :]

    ts_buf[...] = (tx_ref[...] * scale_t).astype(BF16)
    own_cols = pl.ds(pl.multiple_of(z * 128, 128), 128)
    text_sends = []
    for s in range(4):
        copy = remote(
            ts_buf.at[:, pl.ds(s * 128, 128)],
            txt.at[pl.ds(pl.multiple_of(c * SHARE, 16), SHARE), own_cols],
            a2a_sems.at[0, 0, s], a2a_sems.at[0, 1, c % 4], text_to[s],
        )
        copy.start()
        text_sends.append(copy)
    started.append(lambda: [copy.wait_send() for copy in text_sends])

    def rows_of(xx):
        return pl.ds(pl.multiple_of((xx // 2) * SHARE, 16), SHARE)

    def lanes_of(g, xx):
        return pl.ds(pl.multiple_of(g * 256 + (xx % 2) * 128, 128), 128)

    im_low = (im_ref[...] * scale_i).astype(BF16)
    for g in range(4):
        img[y, rows_of(x), lanes_of(g, x)] = im_low[:, g * 128 : g * 128 + 128]

    ways = [[(0, 0, 2), (1, 0, 1)], [(1, 0, 2), (0, 0, 1)]]

    def gather_of(g, phase):
        sems = (g_sems.at[0, g, phase], g_sems.at[1, g, phase])
        if (g + phase) % 2 == 0:
            if phase == 0:
                piece = lambda o, h: img.at[y, rows_of(o), lanes_of(g, o)]
            else:
                piece = lambda o, h: img.at[:, rows_of(o), lanes_of(g, o)]
            return Direct(piece, x, on_x, *sems) if phase == 0 else Gather(piece, x, 4, x_near, ways[g // 2], *sems)
        if phase == 0:
            piece = lambda o, h: img.at[o, rows_of(x), lanes_of(g, x)]
        else:
            piece = lambda o, h: img.at[o, :, pl.ds(g * 256, 256)]
        return Direct(piece, y, on_y, *sems) if phase == 0 else Gather(piece, y, 4, y_near, ways[g // 2], *sems)

    first = [gather_of(g, 0) for g in range(4)]
    second = [gather_of(g, 1) for g in range(4)]

    def text_rows(half, o, h=None):
        start, size = (half * 576, 576) if h is None else (half * 576 + h * 288, 288)
        return txt.at[pl.ds(pl.multiple_of(start, 16), size), pl.ds(pl.multiple_of(o * 128, 128), 128)]

    z_ways = [(0, 0, 4), (1, 1, 4), (1, 0, 3), (0, 1, 3)]
    gz = Gather(lambda o, h: text_rows(fh, o, h), z, 8, z_near, z_ways, gz_sems.at[0], gz_sems.at[1])
    sib_copies = []

    def to_sibling(o, h, slot):
        ref = text_rows(fh, o, h)
        copy = remote(ref, ref, sib_sems.at[0, slot], sib_sems.at[1, slot], sibling)
        copy.start()
        sib_copies.append(copy)

    def from_sibling(o, h, slot):
        ref = text_rows(1 - fh, o, h)
        remote(ref, ref, sib_sems.at[0, slot], sib_sems.at[1, slot], sibling).wait_recv()

    def turn(o):
        cols = pl.ds(pl.multiple_of(o * 128, 128), 128)
        txt_t[cols, :] = txt[:, cols].T

    def turn_step(t):
        for chain in gz.chains(t):
            way, half, n, base = chain
            from_sibling(gz.at(-t - 1 if way == 0 else t + 1), half, base + t)
        turn(gz.at(t + 1))
        if t < 3:
            turn(gz.at(-t - 1))

    lead, trail = [(0, 0), (1, 1)], [(1, 0), (0, 1)]
    for i in range(4):
        ref = txt.at[pl.ds(pl.multiple_of(fh * 576 + i * SHARE, 16), SHARE), own_cols]
        remote(ref, ref, a2a_sems.at[0, 0, i], a2a_sems.at[0, 1, i], sibling).wait_recv()
    far = [[(g // 2, 0)] for g in range(4)]
    near = [[(1 - g // 2, 0)] for g in range(4)]
    gz.send(lead)
    for ring in first:
        ring.send()
    to_sibling(z, None, 14)
    gz.send(trail)
    gz.arrive(0, to_sibling, lead)
    gz.arrive(0, to_sibling, trail)
    for g in range(4):
        first[g].arrive()
        second[g].send(far[g])
    gz.arrive(1, to_sibling, lead)
    from_sibling(z, None, 14)
    turn(z)
    gz.arrive(1, to_sibling, trail)
    for g in range(4):
        second[g].send(near[g])
    turn_step(0)
    gz.arrive(2, to_sibling, lead)
    second[0].arrive(0, None, far[0])
    second[1].arrive(0, None, far[1])
    second[2].arrive(0, None, far[2])
    second[3].arrive(0, None, far[3])
    gz.arrive(2, to_sibling, trail)
    turn_step(1)
    gz.arrive(3, to_sibling)
    turn_step(2)
    second[0].arrive(0, None, near[0])
    second[1].arrive(0, None, near[1])
    second[0].arrive(1)
    second[1].arrive(1)

    temper = jnp.exp(knob_ref[0:1, :])
    bias_value = knob_ref[1:2, :]
    sum_buf[0] = jnp.zeros((3, 8, 128), F32)

    def fold(v):
        v = jnp.sum(v.reshape(32, 8, 256), axis=0)
        return v[:, 0:128] + v[:, 128:256]

    def fold_growth(e):
        e = e.reshape(32, 8, 256)
        while e.shape[0] > 1:
            half = e.shape[0] // 2
            e = e[:half] + e[half:] + e[:half] * e[half:]
        one, two = e[0, :, 0:128], e[0, :, 128:256]
        return one + two + one * two

    def tile(g, p, labels_far):
        o_1 = (z + 7 - p) % 8 if labels_far else z
        o_2 = (z + 1 + p) % 8
        rows_1 = pl.ds(pl.multiple_of(o_1 * 128, 128), 128)
        rows_2 = pl.ds(pl.multiple_of(o_2 * 128, 128), 128)
        cols = pl.ds(pl.multiple_of(g * 256, 256), 256)
        images = img[:, :, cols].reshape(FEATURES, 256)
        texts = jnp.concatenate([txt_t[rows_1, :], txt_t[rows_2, :]], axis=0)

        def finish(labelled):
            scores = jnp.dot(texts, images, preferred_element_type=F32)
            logits = temper * scores + bias_value
            if labelled:
                row = lax.broadcasted_iota(jnp.int32, (256, 256), 0)
                col = lax.broadcasted_iota(jnp.int32, (256, 256), 1)
                same = col == row + xlo * 128
                same = jnp.logical_and(same, row < 128)
                logits = jnp.where(same, -logits, logits)
            e = jnp.exp(-jnp.abs(logits))
            r = 1.0 / (1.0 + e)
            slopes = jnp.where(logits >= 0, r, e * r)
            if labelled:
                slopes = jnp.where(same, -slopes, slopes)
            low = (temper * slopes).astype(BF16)
            wgt[rows_1, cols] = low[0:128]
            wgt[rows_2, cols] = low[128:256]
            sum_buf[0, 0] += fold(jnp.maximum(logits, 0.0)) + jnp.log1p(fold_growth(e))
            sum_buf[0, 1] += fold(slopes * scores)
            sum_buf[0, 2] += fold(slopes)

        if labels_far:
            finish(False)
        else:
            labelled = jnp.logical_and(c // 4 == k, c % 4 == g)
            pl.when(labelled)(lambda: finish(True))
            pl.when(jnp.logical_not(labelled))(lambda: finish(False))

    def early_tiles(g):
        def body(p, _):
            tile(g, p, True)
            return 0

        lax.fori_loop(0, 3, body, 0)

    def image_part(g):
        part = jnp.dot(txt[...], wgt[:, g * 256 : g * 256 + 256], preferred_element_type=F32)
        for yy in range(4):
            for xx in range(4):
                row = yy * 288 + (xx // 2) * SHARE
                piece = part[row : row + SHARE, (xx % 2) * 128 : (xx % 2) * 128 + 128]
                if g % 2 == 0:
                    gi[g, yy, xx] = piece
                else:
                    gi[g, xx, yy] = piece

    def scatter_of(g, phase):
        sems = (s_sems.at[0, g, phase], s_sems.at[1, g, phase])
        even = g % 2 == 0
        if phase == 0:
            ring = (y, 4, y_near) if even else (x, 4, x_near)
            return Scatter(lambda o, h: gi.at[g, o], *ring, ways[g // 2], *sems, land_1.at[g])
        ring = (x, on_x) if even else (y, on_y)
        return Direct(lambda o, h: gi.at[g, y if even else x, o], *ring, *sems, land_2.at[g])

    back_1 = [scatter_of(g, 0) for g in range(4)]
    back_2 = [scatter_of(g, 1) for g in range(4)]

    early_tiles(0)
    early_tiles(1)
    turn_step(3)
    tile(0, 3, False)
    tile(1, 3, False)
    for g in (2, 3):
        second[g].arrive(0, None, near[g])
        second[g].arrive(1)
    early_tiles(2)
    tile(2, 3, False)
    early_tiles(3)
    tile(3, 3, False)

    def total_stage(stage, base, peers):
        copies = []
        for i, peer in enumerate(peers):
            copies.append(remote(
                sum_buf.at[base], sum_buf.at[base + 1 + i],
                total_sems.at[0, stage, i], total_sems.at[1, stage, i], peer,
            ))
        for copy in copies:
            copy.start()

        def done():
            for copy in copies:
                copy.wait()
            total = sum_buf[base]
            for i in range(len(peers)):
                total = total + sum_buf[base + 1 + i]
            sum_buf[base + 1 + len(peers)] = total

        return done

    s_sib = total_stage(0, 0, [sibling])

    own_half = pl.ds(pl.multiple_of(fh * 576, 8), 576)
    sib_half = pl.ds(pl.multiple_of((1 - fh) * 576, 8), 576)
    pairs = [(4, 3), (-3, 2), (-2, 1), (-1, 0)]
    pair_copies = []

    def text_part(q):
        o_1, o_2 = (z + pairs[q][0] + 8) % 8, (z + pairs[q][1] + 8) % 8
        rows_1 = pl.ds(pl.multiple_of(o_1 * 128, 128), 128)
        rows_2 = pl.ds(pl.multiple_of(o_2 * 128, 128), 128)
        weights = jnp.concatenate([wgt[rows_1, :], wgt[rows_2, :]], axis=0)
        part = lax.dot_general(img[...].reshape(FEATURES, 1024), weights, NT, preferred_element_type=F32)
        gt[2 * q] = part[:, 0:128]
        gt[2 * q + 1] = part[:, 128:256]
        copy = remote(
            gt.at[pl.ds(2 * q, 2), sib_half, :], sib_buf.at[pl.ds(2 * q, 2)],
            pair_sems.at[0, q], pair_sems.at[1, q], sibling,
        )
        copy.start()
        pair_copies.append(copy)

    def join(q):
        pair_copies[q].wait_recv()
        for i in (2 * q, 2 * q + 1):
            gt[i, own_half] = gt[i, own_half] + sib_buf[i]

    offsets = [o % 8 for pair in pairs for o in pair]

    sz = Scatter(
        lambda o, h: gt.at[offsets.index(o), pl.ds(pl.multiple_of(fh * 576 + h * 288, 8), 288)],
        0, 8, z_near, z_ways, sz_sems.at[0], sz_sems.at[1], land_z,
    )

    gs = Gather(
        lambda o, h: sum_z.at[o], z, 8, z_near, [(0, 0, 4), (1, 0, 3)], gs_sems.at[0], gs_sems.at[1]
    )
    text_part(0)
    text_part(1)
    image_part(0)
    back_1[0].send()
    join(0)
    sz.send(lead)
    s_sib()
    s_x = total_stage(1, 2, [x_other])
    image_part(1)
    back_1[1].send()
    sz.send([(0, 1)])
    join(1)
    sz.send([(1, 0)])
    text_part(2)
    s_x()
    sum_z[z] = sum_buf[4]
    gs.send()
    image_part(2)
    back_1[2].send()
    sz.arrive(0, lead)
    text_part(3)
    back_1[0].arrive(0, far[0])
    image_part(3)
    back_1[3].send()
    join(2)
    sz.arrive(0, trail)
    gs.arrive(0)
    back_1[1].arrive(0, far[1])
    join(3)
    sz.arrive(1, lead)
    gs.arrive(1)
    back_1[0].arrive(0, near[0])
    back_1[1].arrive(0, near[1])
    back_1[2].arrive(0, far[2])
    sz.arrive(1, trail)
    gs.arrive(2)
    back_1[3].arrive(0, far[3])
    for ring in first + second + [gz]:
        ring.finish()
    for copy in sib_copies:
        copy.wait_send()
    sz.arrive(2, lead)
    gs.arrive(3)
    total = sum_z[0]
    for i in range(1, 8):
        total = total + sum_z[i]
    sum_buf[5] = total
    s_col = total_stage(2, 5, col_peers)
    back_1[0].arrive(1)
    back_2[0].send()
    back_1[1].arrive(1)
    back_2[1].send()
    sz.arrive(2, trail)
    back_1[2].arrive(0, near[2])
    back_1[3].arrive(0, near[3])
    back_1[2].arrive(1)
    back_2[2].send()
    s_col()
    total = sum_buf[13]
    pairs_inv = 1.0 / float(16384 * 16384)
    for i in range(3):
        mean = jnp.sum(jnp.sum(total[i], axis=0, keepdims=True), axis=1, keepdims=True) * pairs_inv
        mean_ref[i : i + 1, :] = jnp.broadcast_to(mean, (1, 128)) * (temper[:, 0:128] if i == 1 else 1.0)
    sz.arrive(3)

    back = []
    for i in range(4):
        copy = remote(
            gt.at[7, pl.ds(pl.multiple_of(fh * 576 + i * SHARE, 8), SHARE), :],
            tg.at[:, pl.ds(pl.multiple_of((c % 4) * 128, 128), 128)],
            a2a_sems.at[1, 0, i], a2a_sems.at[1, 1, c % 4], text_from[i],
        )
        copy.start()
        back.append(copy)
    back_1[3].arrive(1)
    back_2[3].send()

    def image_sum(g):
        return gi[g, y, x] if g % 2 == 0 else gi[g, x, y]

    def image_dot(g):
        back_2[g].arrive()
        cols = slice(g * 128, g * 128 + 128)
        unit = im_ref[:, cols] * scale_buf[0:1, cols]
        dot_buf[0, c, 0:1, cols] = jnp.sum(unit * image_sum(g), axis=0, keepdims=True)

    image_dot(0)
    image_dot(1)
    for s in range(4):
        ref = tg.at[:, pl.ds(s * 128, 128)]
        remote(ref, ref, a2a_sems.at[1, 0, s], a2a_sems.at[1, 1, s], sibling).wait_recv()
    dot_buf[1, c, 0:1, :] = jnp.sum(tx_ref[...] * scale_buf[1:2, :] * tg[...], axis=0, keepdims=True)
    text_dots = over_col(dot_buf.at[1], 2)
    image_dot(2)
    image_dot(3)
    image_dots = over_col(dot_buf.at[0], 1)
    for copy in pair_copies + back:
        copy.wait_send()
    for ring in back_1 + back_2 + [sz, gs]:
        ring.finish()
    dots = text_dots()
    scale_t = scale_buf[1:2, :]
    gt_ref[...] = scale_t * (tg[...] - tx_ref[...] * scale_t * dots[0:1, :])
    dots = image_dots()
    for g in range(4):
        cols = slice(g * 128, g * 128 + 128)
        scale = scale_buf[0:1, cols]
        gi_ref[:, cols] = scale * (image_sum(g) - im_ref[:, cols] * scale * dots[0:1, cols])

    finish_all(started)


def hand_over(mean_ref, gi_in, gt_in, loss_ref, gi_out, gt_out, glt_ref, gb_ref, sems):
    copies = [
        pltpu.make_async_copy(gi_in, gi_out, sems.at[0]),
        pltpu.make_async_copy(gt_in, gt_out, sems.at[1]),
    ]
    for copy in copies:
        copy.start()
    loss_ref[0] = mean_ref[0, 0]
    glt_ref[0] = mean_ref[1, 0]
    gb_ref[0] = mean_ref[2, 0]
    for copy in copies:
        copy.wait()


def per_device(images, texts, log_temp, bias, cid=0, name="contrastive"):
    vmem = pl.BlockSpec(memory_space=pltpu.VMEM)
    smem = pl.BlockSpec(memory_space=pltpu.SMEM)
    anywhere = pl.BlockSpec(memory_space=pl.ANY)
    one = jax.ShapeDtypeStruct((1,), F32)
    grad = jax.ShapeDtypeStruct((SHARE, PAIRS), F32)
    scratch = [
        pltpu.VMEM((8, 8, PAIRS), F32),
        pltpu.VMEM((2, 8, 8, PAIRS), F32),
        pltpu.VMEM((8, PAIRS), F32),
        pltpu.VMEM((SHARE, PAIRS), BF16),
        pltpu.VMEM((4, 2 * SHARE, 1024), BF16),
        pltpu.VMEM((FEATURES, 1024), BF16),
        pltpu.VMEM((1024, FEATURES), BF16),
        pltpu.VMEM((1024, 1024), BF16),
        pltpu.VMEM((4, 4, 4, SHARE, 128), F32),
        pltpu.VMEM((8, FEATURES, 128), F32),
        pltpu.VMEM((8, 576, 128), F32),
        pltpu.VMEM((4, 3, 4, SHARE, 128), F32),
        pltpu.VMEM((4, 3, SHARE, 128), F32),
        pltpu.VMEM((14, 288, 128), F32),
        pltpu.VMEM((14, 3, 8, 128), F32),
        pltpu.VMEM((8, 3, 8, 128), F32),
        pltpu.VMEM((SHARE, PAIRS), F32),
        DMA((3, 2, 7)),
        DMA((2, 2, 4)),
        DMA((2, 15)),
        DMA((2, 4)),
        DMA((2, 4, 2, 3)),
        DMA((2, 14)),
        DMA((2, 4, 2, 3)),
        DMA((2, 14)),
        DMA((2, 7)),
        DMA((2, 3, 7)),
    ]
    row = lax.broadcasted_iota(jnp.int32, (8, 256), 0)
    knobs = jnp.where(row == 0, log_temp, bias)
    means = jax.ShapeDtypeStruct((8, 128), F32)
    parts = pl.pallas_call(
        kernel,
        out_shape=(means, grad, grad),
        in_specs=[vmem] * 3,
        out_specs=[vmem] * 3,
        scratch_shapes=scratch,
        compiler_params=pltpu.CompilerParams(
            collective_id=cid, has_side_effects=True, vmem_limit_bytes=38 * 2**20
        ),
        name=name,
    )(images, texts, knobs)
    return pl.pallas_call(
        hand_over,
        out_shape=(one, grad, grad, one, one),
        in_specs=[vmem] * 3,
        out_specs=[smem, anywhere, anywhere, smem, smem],
        scratch_shapes=[DMA((2,))],
        compiler_params=pltpu.CompilerParams(vmem_limit_bytes=4 * 2**20),
        name="hand_over",
    )(*parts)


def solution(mesh):
    in_specs = (P("col", "blk"), P("col", "blk"), P(), P())
    out_specs = (P(), P("col", "blk"), P("col", "blk"), P(), P())
    return jax.shard_map(
        per_device, mesh=mesh, in_specs=in_specs, out_specs=out_specs, check_vma=False
    )
```

time: 428 us -> 103 us (0.24)
  waiting for transfers between devices: 228 us -> 0 us
  blocking collectives: 133 us -> 0 us
  Pallas kernels: 0 us -> 98.4 us
  matrix products: 24.8 us -> 0 us
  between operations: 21.2 us -> 2.1 us
  starting transfers between devices: 6.63 us -> 0 us
  other arithmetic: 5.81 us -> 0.01 us
  local copies, waits for them, and re-layouts: 7.69 us -> 1.99 us
    psum x3 -> x0, blocking collectives: 122 us -> none  [the longest x1 76.6 us: per_device(): sums_all = lax.psum(sums, ('blk', 'col'))]
    reduce_scatter x2 -> x0, waiting for transfers between devices: 122 us -> none  [the longest x1 122 us: per_device(): lax.psum_scatter(text_part, 'blk', scatter_dimension=1, tiled=True)]
    all_gather x2 -> x0, waiting for transfers between devices: 106 us -> none  [the longest x1 69.3 us: per_device(): text_low = lax.all_gather(text_low, 'blk', axis=1, tiled=True)]
    pallas_call x0 -> x2, Pallas kernels: none -> 98.4 us  [the longest x1 97 us: per_device(): pl.pallas_call(kernel, out_shape=(means, grad, grad), in_specs=[vmem] * 3...]
    dot_general x3 -> x0, matrix products: 24.8 us -> none  [the longest x1 9.89 us: per_device(): lax.dot_general(text_low, image_low, CONTRACT_ROWS, preferred_element_typ...]
    all_to_all x1 -> x0, blocking collectives: 11.2 us -> none  [per_device(): lax.all_to_all(low[1], 'col', split_axis=1, concat_axis=0, tiled=True)]
    all_to_all x1 -> x0, starting transfers between devices: 6.46 us -> none  [per_device(): lax.all_to_all(text_grad, 'col', split_axis=0, concat_axis=1, tiled=True)]
  transfers between devices with their start and end apart: 5 -> 0, of which waited for: 3 -> 0; matrix products, arithmetic and copies ran while one was open for 3% -> 0% of each run, Pallas kernels for 0% -> 0%
where the time goes in v3:
time: 103 us; the launch traced here: 102 us
  Pallas kernels  98.4 us (96%)
  between operations  2.1 us (2%)
  local copies, waits for them, and re-layouts  1.99 us (2%)
    pallas_call x1, Pallas kernels, per_device(): pl.pallas_call(kernel, out_shape=(means, grad, grad), in_specs=[vmem] * 3...  97 us

profile of v3, /device:TPU:2, one launch (start us, length us, event | category | flops | bytes accessed | tf_op | source)
XLA Modules:
  0.0 102.5 jit_solution(10348565617740287945)
XLA Ops:
  1.9 0.1 iota.7.knob_ref
  2.0 0.0 copy-start
  2.0 1.0 copy-done
  3.0 0.0 copy-start.1
  3.0 1.0 copy-done.1
  3.9 97.0 %contrastive.1 = (f32[8,128]{1,0:T(8,128)S(1)}, f32[144,512]{1,0:T(8,128)S(1)}, f32[144,512]{1,0:T(8,128)S(1)}) custom-call(f32[144,512]{1,0:T(8,128)S(1)} %copy-done, f32[144,512]{1,0:T(8,128)S(1)} %copy-done.1, f32[8,256]{1,0:T(8,128)S(1)} %iota.7.knob_ref), custom_call_target="tpu_custom_call" | custom-call | tf_op jit(solution)/shard_map/contrastive/pallas_call | solution.py:632
  101.0 1.4 %hand_over.1 = (f32[1]{0:T(128)}, f32[144,512]{1,0:T(8,128)}, f32[144,512]{1,0:T(8,128)}, f32[1]{0:T(128)}, f32[1]{0:T(128)}) custom-call(f32[8,128]{1,0:T(8,128)S(1)} %get-tuple-element.8.mean_ref, f32[144,512]{1,0:T(8,128)S(1)} %get-tuple-element.9.gi_in, f32[144,512]{1,0:T(8,128)S(1)} %get-tuple-element.10.gt_in), custom_call_target="tpu_custom_call" | custom-call | tf_op jit(solution)/shard_map/hand_over/pallas_call | solution.py:643
  (1 shorter events, 0.0 us)
Async XLA Ops:
  2.0 1.0 copy-start
  3.0 1.0 copy-start.1

commit v4 on v3

v4 whole, which is shorter than its diff:
```python
import functools

import jax
import jax.numpy as jnp
from jax import lax
from jax.experimental import pallas as pl
from jax.experimental.pallas import tpu as pltpu
from jax.sharding import PartitionSpec as P

epsilon = 1e-06
F32 = jnp.float32
BF16 = jnp.bfloat16
MESH = pl.DeviceIdType.MESH
FEATURES = 1152
NT = (((1,), (1,)), ((), ()))
SHARE = 144
PAIRS = 512
DMA = pltpu.SemaphoreType.DMA


def device(x, y, z, core):
    return ((x % 2) * 16 + z * 2 + core, y * 2 + x // 2)


class Ring:
    def __init__(self, piece, place, size, neighbour, chains, sems, whole, landed=None):
        self.piece, self.place, self.size, self.neighbour = piece, place, size, neighbour
        self.sent, self.recvs = sems
        self.whole, self.landed = whole, landed
        self.all = []
        base = 0
        for way, half, n in chains:
            self.all.append((way, half, n, base))
            base += n

    def at(self, offset):
        return (self.place + offset + 2 * self.size) % self.size

    def chains(self, t, only):
        return [chain for chain in self.all if t < chain[2] and (only is None or chain[:2] in only)]

    def remote(self, chain, t, src, dst):
        way, _, _, base = chain
        return pltpu.make_async_remote_copy(
            src_ref=src, dst_ref=dst, send_sem=self.sent, recv_sem=self.recvs.at[base + t],
            device_id=self.neighbour[way], device_id_type=MESH,
        )

    def send(self, only=None):
        for chain in self.chains(0, only):
            self.copy(chain, 0).start()

    def finish(self):
        self.remote(self.all[0], 0, self.whole, self.whole).wait_send()


class Gather(Ring):
    def copy(self, chain, t):
        way, half = chain[:2]
        ref = self.piece(self.at(-t if way == 0 else t), half)
        return self.remote(chain, t, ref, ref)

    def arrive(self, t, only=None, then=None):
        for chain in self.chains(t, only):
            way, half, n, base = chain
            owner = self.at(-t - 1 if way == 0 else t + 1)
            ref = self.piece(owner, half)
            self.remote(chain, t, ref, ref).wait_recv()
            if t + 1 < n:
                self.copy(chain, t + 1).start()
            if then is not None:
                then(owner, 1 + 2 * t + way)


class Scatter(Ring):
    def copy(self, chain, t):
        way, half, n, base = chain
        if t == 0:
            src = self.piece(self.at(n if way == 0 else -n), half)
        else:
            src = self.landed(base + t - 1, half)
        return self.remote(chain, t, src, self.landed(base + t, half))

    def arrive(self, t, only=None):
        for chain in self.chains(t, only):
            way, half, n, base = chain
            self.copy(chain, t).wait_recv()
            ahead = n - t - 1
            own = self.piece(self.at(ahead if way == 0 else -ahead), half)
            slot = self.landed(base + t, half)
            if ahead > 0:
                slot[...] = slot[...] + own[...]
                self.copy(chain, t + 1).start()
            else:
                own[...] = own[...] + slot[...]


class Direct:
    def __init__(self, piece, place, axis, sems, whole, landed=None):
        self.piece, self.place, self.axis = piece, place, axis
        self.sent, self.received = sems
        self.whole, self.landed = whole, landed

    def remote(self, src, dst, i):
        return pltpu.make_async_remote_copy(
            src_ref=src, dst_ref=dst, send_sem=self.sent, recv_sem=self.received,
            device_id=self.axis(i + 1), device_id_type=MESH,
        )

    def send(self):
        for i in (1, 0, 2):
            if self.landed is None:
                src = dst = self.piece(self.place)
            else:
                src, dst = self.piece((self.place + i + 1) % 4), self.landed.at[i]
            self.remote(src, dst, i).start()

    def arrive(self):
        self.remote(self.whole, self.whole, 0).wait_recv()
        if self.landed is not None:
            own = self.piece(self.place)
            own[...] = own[...] + (self.landed[0] + self.landed[1] + self.landed[2])

    def finish(self):
        self.remote(self.whole, self.whole, 0).wait_send()


def finish_all(started):
    for finish in started:
        finish()


def kernel(
    im_ref, tx_ref, knob_ref,
    mean_ref, gi_ref, gt_ref,
    norm_buf, dot_buf, scale_buf, ts_buf, img, txt, txt_t, wgt, gi, gt, sib_buf,
    land_1, land_2, land_z, sum_buf, tg,
    col_sems, a2a_sems, sib_sent, sib_sems, pair_sent, pair_sems, first_sems, g_sent, g_sems, gz_sent, gz_sems,
    s_sent, s_sems, back_sems, sz_sent, sz_sems, total_sems,
):
    b = lax.axis_index("blk")
    c = lax.axis_index("col")
    xlo, z, k = b // 16, (b // 2) % 8, b % 2
    y, xhi = c // 2, c % 2
    x = xhi * 2 + xlo
    fh = 1 - k
    sibling = device(x, y, z, 1 - k)
    x_near = [device((x + 1) % 4, y, z, k), device((x + 3) % 4, y, z, k)]
    y_near = [device(x, (y + 1) % 4, z, k), device(x, (y + 3) % 4, z, k)]
    on_x = lambda i: device((x + i) % 4, y, z, k)
    on_y = lambda i: device(x, (y + i) % 4, z, k)
    z_near = [device(x, y, (z + 1) % 8, k), device(x, y, (z + 7) % 8, k)]
    x_other = device(xhi * 2 + 1 - xlo, y, z, k)
    col_peers = [(b, (c + i) % 8) for i in range(1, 8)]
    across = [(xlo * 16 + z * 2 + 1 - k, 4 * (c // 4) + i) for i in range(4)]
    text_to = [(xlo * 16 + z * 2 + 1 - c // 4, 4 * k + s) for s in range(4)]
    text_from = [(xlo * 16 + z * 2 + c // 4, 4 * fh + i) for i in range(4)]
    started = []

    barrier = pltpu.get_barrier_semaphore()
    greeted = across + x_near + z_near + col_peers
    for peer in greeted:
        pl.semaphore_signal(barrier, inc=1, device_id=peer, device_id_type=MESH)

    def remote(src, dst, send_sem, recv_sem, peer):
        return pltpu.make_async_remote_copy(
            src_ref=src, dst_ref=dst, send_sem=send_sem, recv_sem=recv_sem, device_id=peer, device_id_type=MESH
        )

    im = im_ref[...]
    tx = tx_ref[...]
    norm_buf[c, 0:1, :] = jnp.sum(im * im, axis=0, keepdims=True)
    norm_buf[c, 1:2, :] = jnp.sum(tx * tx, axis=0, keepdims=True)
    pl.semaphore_wait(barrier, len(greeted))

    def over_col(buf, stage):
        for i in range(7):
            remote(buf.at[c], buf.at[c], col_sems.at[stage, 0], col_sems.at[stage, 1], col_peers[i]).start()
        seven = buf.at[pl.ds(0, 7)]
        every = remote(seven, seven, col_sems.at[stage, 0], col_sems.at[stage, 1], col_peers[0])
        started.append(every.wait_send)

        def total():
            every.wait_recv()
            whole = buf[0]
            for i in range(1, 8):
                whole = whole + buf[i]
            return whole

        return total

    scale_buf[...] = lax.rsqrt(over_col(norm_buf, 0)() + epsilon)
    scale_i = scale_buf[0:1, :]
    scale_t = scale_buf[1:2, :]

    ts_buf[...] = (tx_ref[...] * scale_t).astype(BF16)
    own_cols = pl.ds(pl.multiple_of(z * 128, 128), 128)
    for s in range(4):
        remote(
            ts_buf.at[:, pl.ds(s * 128, 128)],
            txt.at[pl.ds(pl.multiple_of(c * SHARE, 16), SHARE), own_cols],
            a2a_sems.at[0, 0], a2a_sems.at[0, 1], text_to[s],
        ).start()
    texts_here = remote(ts_buf, ts_buf, a2a_sems.at[0, 0], a2a_sems.at[0, 1], sibling)
    started.append(texts_here.wait_send)

    def rows_of(xx):
        return pl.ds(pl.multiple_of((xx // 2) * SHARE, 16), SHARE)

    def lanes_of(g, xx):
        return pl.ds(pl.multiple_of(g % 2 * 256 + (xx % 2) * 128, 128), 128)

    im_low = (im_ref[...] * scale_i).astype(BF16)
    for g in range(4):
        img[g // 2, y, rows_of(x), lanes_of(g, x)] = im_low[:, g * 128 : g * 128 + 128]

    ways = [[(0, 0, 2), (1, 0, 1)], [(1, 0, 2), (0, 0, 1)]]
    far = [[(g // 2, 0)] for g in range(4)]
    near = [[(1 - g // 2, 0)] for g in range(4)]

    first_whole = img.at[:, 0, pl.ds(0, SHARE), pl.ds(0, 384)]
    first = [
        Direct(
            lambda o: img.at[:, y, rows_of(o), lanes_of(0, o)], x, on_x,
            (first_sems.at[0, 0], first_sems.at[0, 1]), first_whole,
        ),
        Direct(
            lambda o: img.at[:, o, rows_of(x), lanes_of(1, x)], y, on_y,
            (first_sems.at[1, 0], first_sems.at[1, 1]), first_whole,
        ),
    ]

    def second_of(g):
        sems = (g_sent.at[g], g_sems.at[g])
        whole = img.at[0, pl.ds(0, 3), :, pl.ds(0, 256)]
        if g % 2 == 0:
            piece = lambda o, h: img.at[g // 2, o, :, pl.ds(0, 256)]
            return Gather(piece, y, 4, y_near, ways[g // 2], sems, whole)
        piece = lambda o, h: img.at[g // 2, :, rows_of(o), lanes_of(g, o)]
        return Gather(piece, x, 4, x_near, ways[g // 2], sems, whole)

    second = [second_of(g) for g in range(4)]

    def text_rows(half, o, h=None):
        start, size = (half * 576, 576) if h is None else (half * 576 + h * 288, 288)
        return txt.at[pl.ds(pl.multiple_of(start, 16), size), pl.ds(pl.multiple_of(o * 128, 128), 128)]

    z_ways = [(0, 0, 4), (1, 1, 4), (1, 0, 3), (0, 1, 3)]
    lead, trail = [(0, 0), (1, 1)], [(1, 0), (0, 1)]
    gz = Gather(
        lambda o, h: text_rows(fh, o, h), z, 8, z_near, z_ways, (gz_sent.at[0], gz_sems),
        txt.at[pl.ds(0, 576), pl.ds(0, 896)],
    )

    def to_sibling(o, slot):
        ref = text_rows(fh, o)
        remote(ref, ref, sib_sent.at[0], sib_sems.at[slot], sibling).start()

    def turn(o, slot):
        ref = text_rows(1 - fh, o)
        remote(ref, ref, sib_sent.at[0], sib_sems.at[slot], sibling).wait_recv()
        cols = pl.ds(pl.multiple_of(o * 128, 128), 128)
        txt_t[cols, :] = txt[:, cols].T

    def turn_step(t):
        turn(gz.at(-t - 1), 1 + 2 * t)
        if t < 3:
            turn(gz.at(t + 1), 2 + 2 * t)

    texts_here.wait_recv()
    gz.send(lead)
    for ring in first:
        ring.send()
    gz.send(trail)
    to_sibling(z, 0)
    gz.arrive(0, lead)
    gz.arrive(0, trail, to_sibling)
    first[0].arrive()
    second[0].send(far[0])
    second[2].send(far[2])
    first[1].arrive()
    second[1].send(far[1])
    second[3].send(far[3])
    gz.arrive(1, lead)
    turn(z, 0)
    gz.arrive(1, trail, to_sibling)
    for g in range(4):
        second[g].send(near[g])
    turn_step(0)
    gz.arrive(2, lead)
    for g in range(4):
        second[g].arrive(0, far[g])
    gz.arrive(2, trail, to_sibling)
    turn_step(1)
    gz.arrive(3)
    to_sibling(gz.at(4), 7)
    turn_step(2)
    for g in range(2):
        second[g].arrive(0, near[g])
        second[g].arrive(1)

    temper = jnp.exp(knob_ref[0:1, :])
    bias_value = knob_ref[1:2, :]
    sum_buf[0] = jnp.zeros((3, 8, 128), F32)

    def fold(v):
        v = jnp.sum(v.reshape(32, 8, 256), axis=0)
        return v[:, 0:128] + v[:, 128:256]

    def fold_growth(e):
        e = e.reshape(32, 8, 256)
        while e.shape[0] > 1:
            half = e.shape[0] // 2
            e = e[:half] + e[half:] + e[:half] * e[half:]
        one, two = e[0, :, 0:128], e[0, :, 128:256]
        return one + two + one * two

    def tile(g, p, labels_far):
        o_1 = (z + 7 - p) % 8 if labels_far else z
        o_2 = (z + 1 + p) % 8
        rows_1 = pl.ds(pl.multiple_of(o_1 * 128, 128), 128)
        rows_2 = pl.ds(pl.multiple_of(o_2 * 128, 128), 128)
        cols = pl.ds(pl.multiple_of(g * 256, 256), 256)
        images = img[g // 2, :, :, g % 2 * 256 : g % 2 * 256 + 256].reshape(FEATURES, 256)
        texts = jnp.concatenate([txt_t[rows_1, :], txt_t[rows_2, :]], axis=0)

        def finish(labelled):
            scores = jnp.dot(texts, images, preferred_element_type=F32)
            logits = temper * scores + bias_value
            if labelled:
                row = lax.broadcasted_iota(jnp.int32, (256, 256), 0)
                col = lax.broadcasted_iota(jnp.int32, (256, 256), 1)
                same = col == row + xlo * 128
                same = jnp.logical_and(same, row < 128)
                logits = jnp.where(same, -logits, logits)
            e = jnp.exp(-jnp.abs(logits))
            r = 1.0 / (1.0 + e)
            slopes = jnp.where(logits >= 0, r, e * r)
            if labelled:
                slopes = jnp.where(same, -slopes, slopes)
            low = (temper * slopes).astype(BF16)
            wgt[rows_1, cols] = low[0:128]
            wgt[rows_2, cols] = low[128:256]
            sum_buf[0, 0] += fold(jnp.maximum(logits, 0.0)) + jnp.log1p(fold_growth(e))
            sum_buf[0, 1] += fold(slopes * scores)
            sum_buf[0, 2] += fold(slopes)

        if labels_far:
            finish(False)
        else:
            labelled = jnp.logical_and(c // 4 == k, c % 4 == g)
            pl.when(labelled)(lambda: finish(True))
            pl.when(jnp.logical_not(labelled))(lambda: finish(False))

    def early_tiles(g):
        def body(p, _):
            tile(g, p, True)
            return 0

        lax.fori_loop(0, 3, body, 0)

    def image_part(g):
        part = jnp.dot(txt[...], wgt[:, g * 256 : g * 256 + 256], preferred_element_type=F32)
        for yy in range(4):
            for xx in range(4):
                row = yy * 288 + (xx // 2) * SHARE
                piece = part[row : row + SHARE, (xx % 2) * 128 : (xx % 2) * 128 + 128]
                if g % 2 == 0:
                    gi[g, yy, xx] = piece
                else:
                    gi[g, xx, yy] = piece

    def back_1_of(g):
        ring = (y, 4, y_near) if g % 2 == 0 else (x, 4, x_near)
        return Scatter(
            lambda o, h: gi.at[g, o], *ring, ways[g // 2], (s_sent.at[g], s_sems.at[g]), land_1.at[g],
            lambda i, h: land_1.at[g, i],
        )

    def back_2_of(g):
        ring = (x, on_x) if g % 2 == 0 else (y, on_y)
        return Direct(
            lambda o: gi.at[g, y if g % 2 == 0 else x, o], *ring, (back_sems.at[0, g], back_sems.at[1, g]),
            land_2.at[g], land_2.at[g],
        )

    back_1 = [back_1_of(g) for g in range(4)]
    back_2 = [back_2_of(g) for g in range(4)]

    early_tiles(0)
    early_tiles(1)
    turn_step(3)
    tile(0, 3, False)
    tile(1, 3, False)
    for g in (2, 3):
        second[g].arrive(0, near[g])
        second[g].arrive(1)
    early_tiles(2)
    tile(2, 3, False)
    early_tiles(3)
    tile(3, 3, False)

    def total_stage(stage, base, peers):
        copies = []
        for i, peer in enumerate(peers):
            copies.append(remote(
                sum_buf.at[base], sum_buf.at[base + 1 + i],
                total_sems.at[0, stage, i], total_sems.at[1, stage, i], peer,
            ))
        for copy in copies:
            copy.start()

        def done():
            for copy in copies:
                copy.wait()
            total = sum_buf[base]
            for i in range(len(peers)):
                total = total + sum_buf[base + 1 + i]
            sum_buf[base + 1 + len(peers)] = total

        return done

    s_sib = total_stage(0, 0, [sibling])

    own_half = pl.ds(pl.multiple_of(fh * 584 + 8, 8), 576)
    sib_half = pl.ds(pl.multiple_of((1 - fh) * 584 + 8, 8), 576)
    sum_rows = pl.ds(pl.multiple_of(fh * 584, 8), 8)
    pairs = [(4, 3), (-3, 2), (-2, 1), (-1, 0)]

    def text_part(q):
        o_1, o_2 = (z + pairs[q][0] + 8) % 8, (z + pairs[q][1] + 8) % 8
        rows_1 = pl.ds(pl.multiple_of(o_1 * 128, 128), 128)
        rows_2 = pl.ds(pl.multiple_of(o_2 * 128, 128), 128)
        weights = jnp.concatenate([wgt[rows_1, :], wgt[rows_2, :]], axis=0)
        part = lax.dot_general(
            img[0].reshape(FEATURES, 512), weights[:, 0:512], NT, preferred_element_type=F32
        ) + lax.dot_general(img[1].reshape(FEATURES, 512), weights[:, 512:1024], NT, preferred_element_type=F32)
        for i in range(2):
            for f in range(2):
                gt[2 * q + i, f * 584 + 8 : f * 584 + 584] = part[f * 576 : f * 576 + 576, i * 128 : i * 128 + 128]
        pair_copy(q).start()

    def pair_copy(q):
        return remote(
            gt.at[pl.ds(2 * q, 2), sib_half, :], sib_buf.at[pl.ds(2 * q, 2)],
            pair_sent.at[0], pair_sems.at[q], sibling,
        )

    def join(q):
        pair_copy(q).wait_recv()
        for i in (2 * q, 2 * q + 1):
            gt[i, own_half] = gt[i, own_half] + sib_buf[i]

    offsets = [o % 8 for pair in pairs for o in pair]

    def gt_piece(o, h):
        rows = pl.ds(pl.multiple_of(fh * 584, 8), 296) if h == 0 else pl.ds(pl.multiple_of(fh * 584 + 296, 8), 288)
        return gt.at[offsets.index(o), rows]

    sz = Scatter(
        gt_piece, 0, 8, z_near, z_ways, (sz_sent.at[0], sz_sems), gt.at[pl.ds(0, 7), pl.ds(0, 584)],
        lambda i, h: land_z.at[i, pl.ds(0, 296 if h == 0 else 288)],
    )
    text_part(0)
    s_sib()
    s_x = total_stage(1, 2, [x_other])
    image_part(0)
    back_1[0].send()
    image_part(1)
    back_1[1].send()
    s_x()
    sums = jnp.concatenate([jnp.sum(sum_buf[4, i], axis=0, keepdims=True) for i in range(3)] * 2 + [jnp.zeros((2, 128), F32)])
    for i in range(8):
        gt[i, sum_rows] = sums
    join(0)
    sz.send(lead)
    text_part(1)
    sz.send([(0, 1)])
    image_part(2)
    back_1[2].send()
    join(1)
    sz.send([(1, 0)])
    image_part(3)
    back_1[3].send()
    text_part(2)
    sz.arrive(0, lead)
    back_1[0].arrive(0, far[0])
    text_part(3)
    join(2)
    sz.arrive(0, trail)
    back_1[1].arrive(0, far[1])
    join(3)
    sz.arrive(1, lead)
    back_1[2].arrive(0, far[2])
    back_1[3].arrive(0, far[3])
    sz.arrive(1, trail)
    back_1[0].arrive(0, near[0])
    back_1[1].arrive(0, near[1])
    sz.arrive(2, lead)
    back_1[0].arrive(1)
    back_2[0].send()
    back_1[1].arrive(1)
    back_2[1].send()
    sz.arrive(2, trail)
    back_1[2].arrive(0, near[2])
    back_1[3].arrive(0, near[3])
    back_1[2].arrive(1)
    back_2[2].send()
    sz.arrive(3)

    for i in range(4):
        remote(
            gt.at[7, pl.ds(pl.multiple_of(fh * 584 + 8 + i * SHARE, 8), SHARE), :],
            tg.at[:, pl.ds(pl.multiple_of((c % 4) * 128, 128), 128)],
            a2a_sems.at[1, 0], a2a_sems.at[1, 1], text_from[i],
        ).start()
    grads_here = remote(tg, tg, a2a_sems.at[1, 0], a2a_sems.at[1, 1], sibling)
    started.append(grads_here.wait_send)
    back_1[3].arrive(1)
    back_2[3].send()

    def image_sum(g):
        return gi[g, y, x] if g % 2 == 0 else gi[g, x, y]

    def image_dot(g):
        back_2[g].arrive()
        cols = slice(g * 128, g * 128 + 128)
        unit = im_ref[:, cols] * scale_buf[0:1, cols]
        dot_buf[c, 0:1, cols] = jnp.sum(unit * image_sum(g), axis=0, keepdims=True)

    dot_buf[c, 2:5, 0:128] = gt[7, sum_rows][0:3]
    image_dot(0)
    image_dot(1)
    grads_here.wait_recv()
    dot_buf[c, 1:2, :] = jnp.sum(tx_ref[...] * scale_buf[1:2, :] * tg[...], axis=0, keepdims=True)
    image_dot(2)
    image_dot(3)
    every_dot = over_col(dot_buf, 1)
    pairs_sent = remote(sib_buf, sib_buf, pair_sent.at[0], pair_sems.at[0], sibling)
    texts_sent = remote(txt.at[pl.ds(0, 576), :], txt.at[pl.ds(0, 576), :], sib_sent.at[0], sib_sems.at[0], sibling)
    for copy in (pairs_sent, texts_sent):
        copy.wait_send()
    for ring in first + second + [gz] + back_1 + back_2 + [sz]:
        ring.finish()
    dots = every_dot()
    scale_t = scale_buf[1:2, :]
    gt_ref[...] = scale_t * (tg[...] - tx_ref[...] * scale_t * dots[1:2, :])
    for g in range(4):
        cols = slice(g * 128, g * 128 + 128)
        scale = scale_buf[0:1, cols]
        gi_ref[:, cols] = scale * (image_sum(g) - im_ref[:, cols] * scale * dots[0:1, cols])
    means = jnp.sum(dots[:, 0:128], axis=1, keepdims=True) * (1.0 / float(16384 * 16384))
    mean_ref[...] = jnp.broadcast_to(means, (8, 128))
    mean_ref[3:4, :] = mean_ref[3:4, :] * temper[:, 0:128]

    finish_all(started)


def hand_over(mean_ref, gi_in, gt_in, loss_ref, gi_out, gt_out, glt_ref, gb_ref, sems):
    copies = [
        pltpu.make_async_copy(gi_in, gi_out, sems.at[0]),
        pltpu.make_async_copy(gt_in, gt_out, sems.at[1]),
    ]
    for copy in copies:
        copy.start()
    loss_ref[0] = mean_ref[2, 0]
    glt_ref[0] = mean_ref[3, 0]
    gb_ref[0] = mean_ref[4, 0]
    for copy in copies:
        copy.wait()


def per_device(images, texts, log_temp, bias, cid=0, name="contrastive"):
    vmem = pl.BlockSpec(memory_space=pltpu.VMEM)
    smem = pl.BlockSpec(memory_space=pltpu.SMEM)
    anywhere = pl.BlockSpec(memory_space=pl.ANY)
    one = jax.ShapeDtypeStruct((1,), F32)
    grad = jax.ShapeDtypeStruct((SHARE, PAIRS), F32)
    scratch = [
        pltpu.VMEM((8, 8, PAIRS), F32),
        pltpu.VMEM((8, 8, PAIRS), F32),
        pltpu.VMEM((8, PAIRS), F32),
        pltpu.VMEM((SHARE, PAIRS), BF16),
        pltpu.VMEM((2, 4, 2 * SHARE, 512), BF16),
        pltpu.VMEM((FEATURES, 1024), BF16),
        pltpu.VMEM((1024, FEATURES), BF16),
        pltpu.VMEM((1024, 1024), BF16),
        pltpu.VMEM((4, 4, 4, SHARE, 128), F32),
        pltpu.VMEM((8, 1168, 128), F32),
        pltpu.VMEM((8, 576, 128), F32),
        pltpu.VMEM((4, 3, 4, SHARE, 128), F32),
        pltpu.VMEM((4, 3, SHARE, 128), F32),
        pltpu.VMEM((14, 296, 128), F32),
        pltpu.VMEM((5, 3, 8, 128), F32),
        pltpu.VMEM((SHARE, PAIRS), F32),
        DMA((2, 2)),
        DMA((2, 2)),
        DMA((1,)),
        DMA((8,)),
        DMA((1,)),
        DMA((4,)),
        DMA((2, 2)),
        DMA((4,)),
        DMA((4, 3)),
        DMA((1,)),
        DMA((14,)),
        DMA((4,)),
        DMA((4, 3)),
        DMA((2, 4)),
        DMA((1,)),
        DMA((14,)),
        DMA((2, 2, 1)),
    ]
    row = lax.broadcasted_iota(jnp.int32, (8, 256), 0)
    knobs = jnp.where(row == 0, log_temp, bias)
    means = jax.ShapeDtypeStruct((8, 128), F32)
    parts = pl.pallas_call(
        kernel,
        out_shape=(means, grad, grad),
        in_specs=[vmem] * 3,
        out_specs=[vmem] * 3,
        scratch_shapes=scratch,
        compiler_params=pltpu.CompilerParams(
            collective_id=cid, has_side_effects=True, vmem_limit_bytes=38 * 2**20
        ),
        name=name,
    )(images, texts, knobs)
    return pl.pallas_call(
        hand_over,
        out_shape=(one, grad, grad, one, one),
        in_specs=[vmem] * 3,
        out_specs=[smem, anywhere, anywhere, smem, smem],
        scratch_shapes=[DMA((2,))],
        compiler_params=pltpu.CompilerParams(vmem_limit_bytes=4 * 2**20),
        name="hand_over",
    )(*parts)


def solution(mesh):
    in_specs = (P("col", "blk"), P("col", "blk"), P(), P())
    out_specs = (P(), P("col", "blk"), P("col", "blk"), P(), P())
    return jax.shard_map(
        per_device, mesh=mesh, in_specs=in_specs, out_specs=out_specs, check_vma=False
    )
```

time: 103 us -> 93.6 us (0.909)
  Pallas kernels: 98.4 us -> 88.8 us
    pallas_call x1, Pallas kernels: 97 us -> 87.4 us  [per_device(): pl.pallas_call(kernel, out_shape=(means, grad, grad), in_specs=[vmem] * 3...]
where the time goes in v4:
time: 93.6 us; the launch traced here: 92.9 us
  Pallas kernels  88.8 us (95%)
  between operations  2.1 us (2%)
  local copies, waits for them, and re-layouts  1.99 us (2%)
    pallas_call x1, Pallas kernels, per_device(): pl.pallas_call(kernel, out_shape=(means, grad, grad), in_specs=[vmem] * 3...  87.4 us
    unnamed x4, local copies, waits for them, and re-layouts  1.92 us

profile of v4, /device:TPU:2, one launch (start us, length us, event | category | flops | bytes accessed | tf_op | source)
XLA Modules:
  0.0 92.9 jit_solution(17258062573595473347)
XLA Ops:
  1.9 0.1 iota.7.knob_ref
  2.0 0.0 copy-start
  2.0 1.0 %copy-done = f32[144,512]{1,0:T(8,128)S(1)} copy-done((f32[144,512]{1,0:T(8,128)S(1)}, f32[144,512]{1,0:T(8,128)}, u32[]{:S(2)}) %copy-start) | copy-done | bytes 294936
  3.0 0.0 copy-start.1
  3.0 1.0 %copy-done.1 = f32[144,512]{1,0:T(8,128)S(1)} copy-done((f32[144,512]{1,0:T(8,128)S(1)}, f32[144,512]{1,0:T(8,128)}, u32[]{:S(2)}) %copy-start.1) | copy-done | bytes 294936
  3.9 87.4 %contrastive.1 = (f32[8,128]{1,0:T(8,128)S(1)}, f32[144,512]{1,0:T(8,128)S(1)}, f32[144,512]{1,0:T(8,128)S(1)}) custom-call(f32[144,512]{1,0:T(8,128)S(1)} %copy-done, f32[144,512]{1,0:T(8,128)S(1)} %copy-done.1, f32[8,256]{1,0:T(8,128)S(1)} %iota.7.knob_ref), custom_call_target="tpu_custom_call" | custom-call | tf_op jit(solution)/shard_map/contrastive/pallas_call | solution.py:617
  91.3 1.4 %hand_over.1 = (f32[1]{0:T(128)}, f32[144,512]{1,0:T(8,128)}, f32[144,512]{1,0:T(8,128)}, f32[1]{0:T(128)}, f32[1]{0:T(128)}) custom-call(f32[8,128]{1,0:T(8,128)S(1)} %get-tuple-element.8.mean_ref, f32[144,512]{1,0:T(8,128)S(1)} %get-tuple-element.9.gi_in, f32[144,512]{1,0:T(8,128)S(1)} %get-tuple-element.10.gt_in), custom_call_target="tpu_custom_call" | custom-call | tf_op jit(solution)/shard_map/hand_over/pallas_call | solution.py:628
  (1 shorter events, 0.0 us)
Async XLA Ops:
  2.0 1.0 %copy-start = (f32[144,512]{1,0:T(8,128)S(1)}, f32[144,512]{1,0:T(8,128)}, u32[]{:S(2)}) copy-start(f32[144,512]{1,0:T(8,128)} %im_ref.1) | copy-start | bytes 884740
  3.0 1.0 %copy-start.1 = (f32[144,512]{1,0:T(8,128)S(1)}, f32[144,512]{1,0:T(8,128)}, u32[]{:S(2)}) copy-start(f32[144,512]{1,0:T(8,128)} %tx_ref.1) | copy-start | bytes 884740

commit v5 on v4

--- a/solution.py
+++ b/solution.py
@@ -134,7 +134,7 @@
     im_ref, tx_ref, knob_ref,
     mean_ref, gi_ref, gt_ref,
     norm_buf, dot_buf, scale_buf, ts_buf, img, txt, txt_t, wgt, gi, gt, sib_buf,
-    land_1, land_2, land_z, sum_buf, tg,
+    land_1, land_2, land_z, tile_sums, sum_buf, tg,
     col_sems, a2a_sems, sib_sent, sib_sems, pair_sent, pair_sems, first_sems, g_sent, g_sems, gz_sent, gz_sems,
     s_sent, s_sems, back_sems, sz_sent, sz_sems, total_sems,
 ):
@@ -267,10 +267,10 @@
         if t < 3:
             turn(gz.at(t + 1), 2 + 2 * t)
 
+    for ring in first:
+        ring.send()
     texts_here.wait_recv()
     gz.send(lead)
-    for ring in first:
-        ring.send()
     gz.send(trail)
     to_sibling(z, 0)
     gz.arrive(0, lead)
@@ -301,7 +301,7 @@
 
     temper = jnp.exp(knob_ref[0:1, :])
     bias_value = knob_ref[1:2, :]
-    sum_buf[0] = jnp.zeros((3, 8, 128), F32)
+    tile_sums[...] = jnp.zeros_like(tile_sums)
 
     def fold(v):
         v = jnp.sum(v.reshape(32, 8, 256), axis=0)
@@ -341,9 +341,9 @@
             low = (temper * slopes).astype(BF16)
             wgt[rows_1, cols] = low[0:128]
             wgt[rows_2, cols] = low[128:256]
-            sum_buf[0, 0] += fold(jnp.maximum(logits, 0.0)) + jnp.log1p(fold_growth(e))
-            sum_buf[0, 1] += fold(slopes * scores)
-            sum_buf[0, 2] += fold(slopes)
+            tile_sums[0] += fold(jnp.maximum(logits, 0.0)) + jnp.log1p(fold_growth(e))
+            tile_sums[1] += fold(slopes * scores)
+            tile_sums[2] += fold(slopes)
 
         if labels_far:
             finish(False)
@@ -352,12 +352,12 @@
             pl.when(labelled)(lambda: finish(True))
             pl.when(jnp.logical_not(labelled))(lambda: finish(False))
 
-    def early_tiles(g):
+    def early_tiles(g, start=0, stop=3):
         def body(p, _):
             tile(g, p, True)
             return 0
 
-        lax.fori_loop(0, 3, body, 0)
+        lax.fori_loop(start, stop, body, 0)
 
     def image_part(g):
         part = jnp.dot(txt[...], wgt[:, g * 256 : g * 256 + 256], preferred_element_type=F32)
@@ -395,10 +395,9 @@
     for g in (2, 3):
         second[g].arrive(0, near[g])
         second[g].arrive(1)
-    early_tiles(2)
-    tile(2, 3, False)
-    early_tiles(3)
-    tile(3, 3, False)
+    for g in (2, 3):
+        tile(g, 3, False)
+        early_tiles(g, 2, 3)
 
     def total_stage(stage, base, peers):
         copies = []
@@ -419,8 +418,6 @@
             sum_buf[base + 1 + len(peers)] = total
 
         return done
-
-    s_sib = total_stage(0, 0, [sibling])
 
     own_half = pl.ds(pl.multiple_of(fh * 584 + 8, 8), 576)
     sib_half = pl.ds(pl.multiple_of((1 - fh) * 584 + 8, 8), 576)
@@ -462,19 +459,19 @@
         lambda i, h: land_z.at[i, pl.ds(0, 296 if h == 0 else 288)],
     )
     text_part(0)
-    s_sib()
-    s_x = total_stage(1, 2, [x_other])
+    early_tiles(2, 0, 2)
+    early_tiles(3, 0, 2)
+    sums = [jnp.sum(tile_sums[i], axis=0, keepdims=True) for i in range(3)]
+    sums = jnp.concatenate(sums + [jnp.zeros((5, 128), F32)])
+    for i in range(8):
+        gt[i, sum_rows] = sums
     image_part(0)
     back_1[0].send()
+    text_part(1)
+    join(0)
+    sz.send(lead)
     image_part(1)
     back_1[1].send()
-    s_x()
-    sums = jnp.concatenate([jnp.sum(sum_buf[4, i], axis=0, keepdims=True) for i in range(3)] * 2 + [jnp.zeros((2, 128), F32)])
-    for i in range(8):
-        gt[i, sum_rows] = sums
-    join(0)
-    sz.send(lead)
-    text_part(1)
     sz.send([(0, 1)])
     image_part(2)
     back_1[2].send()
@@ -516,8 +513,12 @@
         ).start()
     grads_here = remote(tg, tg, a2a_sems.at[1, 0], a2a_sems.at[1, 1], sibling)
     started.append(grads_here.wait_send)
+    sum_buf[0] = gt[7, sum_rows]
+    s_sib = total_stage(0, 0, [sibling])
     back_1[3].arrive(1)
     back_2[3].send()
+    s_sib()
+    s_x = total_stage(1, 2, [x_other])
 
     def image_sum(g):
         return gi[g, y, x] if g % 2 == 0 else gi[g, x, y]
@@ -528,11 +529,12 @@
         unit = im_ref[:, cols] * scale_buf[0:1, cols]
         dot_buf[c, 0:1, cols] = jnp.sum(unit * image_sum(g), axis=0, keepdims=True)
 
-    dot_buf[c, 2:5, 0:128] = gt[7, sum_rows][0:3]
     image_dot(0)
     image_dot(1)
     grads_here.wait_recv()
     dot_buf[c, 1:2, :] = jnp.sum(tx_ref[...] * scale_buf[1:2, :] * tg[...], axis=0, keepdims=True)
+    s_x()
+    dot_buf[c, 2:5, 0:128] = sum_buf[4, 0:3]
     image_dot(2)
     image_dot(3)
     every_dot = over_col(dot_buf, 1)
@@ -591,7 +593,8 @@
         pltpu.VMEM((4, 3, 4, SHARE, 128), F32),
         pltpu.VMEM((4, 3, SHARE, 128), F32),
         pltpu.VMEM((14, 296, 128), F32),
-        pltpu.VMEM((5, 3, 8, 128), F32),
+        pltpu.VMEM((3, 8, 128), F32),
+        pltpu.VMEM((5, 8, 128), F32),
         pltpu.VMEM((SHARE, PAIRS), F32),
         DMA((2, 2)),
         DMA((2, 2)),

time: 93.6 us -> 93.3 us (level)
  no operation moved by 1% of the time
where the time goes in v5:
time: 93.3 us; the launch traced here: 92.2 us
  Pallas kernels  88.1 us (94%)
  between operations  2.1 us (2%)
  local copies, waits for them, and re-layouts  1.99 us (2%)
    pallas_call x1, Pallas kernels, per_device(): pl.pallas_call(kernel, out_shape=(means, grad, grad), in_specs=[vmem] * 3...  86.7 us
    unnamed x4, local copies, waits for them, and re-layouts  1.92 us

profile of v5, /device:TPU:2, one launch (start us, length us, event | category | flops | bytes accessed | tf_op | source)
XLA Modules:
  0.0 92.2 jit_solution(2688559558935055604)
XLA Ops:
  1.9 0.1 iota.7.knob_ref
  2.0 0.0 copy-start
  2.0 1.0 %copy-done = f32[144,512]{1,0:T(8,128)S(1)} copy-done((f32[144,512]{1,0:T(8,128)S(1)}, f32[144,512]{1,0:T(8,128)}, u32[]{:S(2)}) %copy-start) | copy-done | bytes 294936
  3.0 0.0 copy-start.1
  3.0 1.0 %copy-done.1 = f32[144,512]{1,0:T(8,128)S(1)} copy-done((f32[144,512]{1,0:T(8,128)S(1)}, f32[144,512]{1,0:T(8,128)}, u32[]{:S(2)}) %copy-start.1) | copy-done | bytes 294936
  3.9 86.7 %contrastive.1 = (f32[8,128]{1,0:T(8,128)S(1)}, f32[144,512]{1,0:T(8,128)S(1)}, f32[144,512]{1,0:T(8,128)S(1)}) custom-call(f32[144,512]{1,0:T(8,128)S(1)} %copy-done, f32[144,512]{1,0:T(8,128)S(1)} %copy-done.1, f32[8,256]{1,0:T(8,128)S(1)} %iota.7.knob_ref), custom_call_target="tpu_custom_call" | custom-call | tf_op jit(solution)/shard_map/contrastive/pallas_call | solution.py:620
  90.7 1.4 %hand_over.1 = (f32[1]{0:T(128)}, f32[144,512]{1,0:T(8,128)}, f32[144,512]{1,0:T(8,128)}, f32[1]{0:T(128)}, f32[1]{0:T(128)}) custom-call(f32[8,128]{1,0:T(8,128)S(1)} %get-tuple-element.8.mean_ref, f32[144,512]{1,0:T(8,128)S(1)} %get-tuple-element.9.gi_in, f32[144,512]{1,0:T(8,128)S(1)} %get-tuple-element.10.gt_in), custom_call_target="tpu_custom_call" | custom-call | tf_op jit(solution)/shard_map/hand_over/pallas_call | solution.py:631
  (1 shorter events, 0.0 us)
Async XLA Ops:
  2.0 1.0 %copy-start = (f32[144,512]{1,0:T(8,128)S(1)}, f32[144,512]{1,0:T(8,128)}, u32[]{:S(2)}) copy-start(f32[144,512]{1,0:T(8,128)} %im_ref.1) | copy-start | bytes 884740
  3.0 1.0 %copy-start.1 = (f32[144,512]{1,0:T(8,128)S(1)}, f32[144,512]{1,0:T(8,128)}, u32[]{:S(2)}) copy-start(f32[144,512]{1,0:T(8,128)} %tx_ref.1) | copy-start | bytes 884740
